TPU v7x, 32 devices: a whole 2x2x4 slice. The times are simulated.
32 devices in a mesh: ep: 8 (over z, x), tp: 4 (over y, core).
Axes of the slice: x: 2, y: 2, z: 4, core: 2. Of those that a mesh axis runs over, the one named last changes fastest.
Arguments:
- tokens: bfloat16 [4096, 1024], P('ep'), may hold values from -6 to 6
- norm_attn: float32 [1024], replicated, may hold values from 0.1 to 1.9
- w_query: bfloat16 [1024, 1024], P(None, 'tp'), may hold values from -0.1875 to 0.1875
- w_key: bfloat16 [1024, 512], P(None, 'tp'), may hold values from -0.1875 to 0.1875
- w_value: bfloat16 [1024, 512], P(None, 'tp'), may hold values from -0.1875 to 0.1875
- w_out: bfloat16 [1024, 1024], P('tp'), may hold values from -2 to 2
- norm_moe: float32 [1024], replicated, may hold values from 0.1 to 1.9
- router: bfloat16 [1024, 32], replicated, may hold values from -0.09375 to 0.09375
- expert_gate: bfloat16 [32, 1024, 512], P('ep', None, 'tp'), may hold values from -0.1875 to 0.1875
- expert_up: bfloat16 [32, 1024, 512], P('ep', None, 'tp'), may hold values from -0.1875 to 0.1875
- expert_down: bfloat16 [32, 512, 1024], P('ep', 'tp'), may hold values from -1 to 1
- lengths: int32 [8, 4], P('ep'), may hold values from 1 to 256, 512 in all within a row
- expert_ids: int32 [4096, 8], P('ep'), may hold values from 0 to 31, all different within a row; in each aligned block of 512 rows (0 to 511, 512 to 1023, ...) at most 192 rows name the same one
- out_grad: bfloat16 [4096, 1024], P('ep'), may hold values from -6 to 6
Outputs:
- output: bfloat16 [4096, 1024], P('ep')
- grad_tokens: bfloat16 [4096, 1024], P('ep')
- grad_norm_attn: float32 [1024], replicated
- grad_w_query: float32 [1024, 1024], P(None, 'tp')
- grad_w_key: float32 [1024, 512], P(None, 'tp')
- grad_w_value: float32 [1024, 512], P(None, 'tp')
- grad_w_out: float32 [1024, 1024], P('tp')
- grad_norm_moe: float32 [1024], replicated
- grad_router: float32 [1024, 32], replicated
- grad_expert_gate: float32 [32, 1024, 512], P('ep', None, 'tp')
- grad_expert_up: float32 [32, 1024, 512], P('ep', None, 'tp')
- grad_expert_down: float32 [32, 512, 1024], P('ep', 'tp')
Inputs may be any that keep to these rules, and one draw needn't show every extreme that they name: Each group's 4 lengths sum to 512; in every group the longest is exactly 256. `expert_ids`: each token names 8 different experts. Among the 512 tokens of one group no expert is named more than 192 times, a bound that some block reaches.
All inputs are finite; a program needn't handle non-finite values.
Results may differ from a plain program's by a relative error of at most 0.02.
Values may be sent and summed in bfloat16 or wider, within the bound.
A program may use at most 256 MiB of HBM per device.

v0:
```python
import jax
import jax.numpy as jnp
from jax import lax
from jax.sharding import PartitionSpec as P

HEAD = 64
EXPERTS = 32
TOP = 8
CAP = 192


EPSILON = 1e-06
ROPE_BASE = 10000.0


def seq_layout(seq_lengths, tok_rows):
    seq_ends = jnp.cumsum(seq_lengths, dtype=jnp.int32)
    seq_starts = seq_ends - seq_lengths
    places = jnp.arange(tok_rows, dtype=jnp.int32)
    segment = jnp.sum(
        (places[:, None] >= seq_ends[None, :]).astype(jnp.int32), axis=1, dtype=jnp.int32
    )
    slot_match = segment[:, None] == jnp.arange(seq_lengths.shape[0], dtype=jnp.int32)[None, :]
    begins = jnp.sum(jnp.where(slot_match, seq_starts[None, :], 0), axis=1, dtype=jnp.int32)
    return (segment, places - begins)


def rope_tables(position, head_size):
    half_width = head_size // 2
    inverse = ROPE_BASE ** (-2.0 * jnp.arange(half_width, dtype=jnp.float32) / head_size)
    angles = position.astype(jnp.float32)[:, None] * inverse[None, :]
    angles = jnp.concatenate([angles, angles], axis=1)
    return (jnp.cos(angles), jnp.sin(angles))


def rotate(values, cosine, sine_part):
    half_width = values.shape[-1] // 2
    turned = jnp.concatenate([-values[..., half_width:], values[..., :half_width]], axis=-1)
    return values * cosine[:, None, :] + turned * sine_part[:, None, :]


def unrotate(grads, cosine, sine_part):
    half_width = grads.shape[-1] // 2
    scaled = grads * sine_part[:, None, :]
    turned = jnp.concatenate([scaled[..., half_width:], -scaled[..., :half_width]], axis=-1)
    return grads * cosine[:, None, :] + turned


def slot_table(expert_ids, expert_count, capacity):
    flat_ids = expert_ids.reshape(-1)
    pair_count = flat_ids.shape[0]
    one_hot = (flat_ids[:, None] == jnp.arange(expert_count, dtype=jnp.int32)[None, :]).astype(
        jnp.int32
    )
    earlier = jnp.cumsum(one_hot, axis=0, dtype=jnp.int32) - one_hot
    ranks = jnp.sum(earlier * one_hot, axis=1, dtype=jnp.int32)
    pair_slot = flat_ids * capacity + ranks
    slot_owner = (
        jnp.full((expert_count * capacity,), pair_count, jnp.int32)
        .at[pair_slot]
        .set(jnp.arange(pair_count, dtype=jnp.int32))
    )
    return (pair_slot, slot_owner)


def to_experts(padded_rows, owner_token, slot_gate):
    model_width = padded_rows.shape[1]
    picked = padded_rows[owner_token]
    if slot_gate is not None:
        picked = slot_gate[:, None] * picked
    buffer = picked.astype(jnp.bfloat16).reshape(EXPERTS, -1, model_width)
    return lax.all_to_all(buffer, "ep", split_axis=0, concat_axis=1, tiled=True)


def to_sources(partial_rows):
    summed = lax.psum_scatter(partial_rows, "tp", scatter_dimension=2, tiled=True).astype(
        jnp.bfloat16
    )
    joined = lax.all_gather(summed, "tp", axis=2, tiled=True)
    return lax.all_to_all(joined, "ep", split_axis=1, concat_axis=0, tiled=True)


def body(
    tokens,
    norm_attn,
    w_query,
    w_key,
    w_value,
    w_out,
    norm_moe,
    router,
    expert_gate,
    expert_up,
    expert_down,
    lengths,
    expert_ids,
    out_grad,
):
    highest = lax.Precision.HIGHEST
    tok_rows, model_width = tokens.shape
    kv_local = w_key.shape[1] // HEAD
    group_size = w_query.shape[1] // w_key.shape[1]
    block_rows = min(512, tok_rows)
    block_count = tok_rows // block_rows
    score_scale = HEAD ** (-0.5)
    x_full = tokens.astype(jnp.float32)
    scale_one = lax.rsqrt(jnp.mean(x_full * x_full, axis=1, keepdims=True) + EPSILON)
    normed_one = (x_full * scale_one * norm_attn).astype(jnp.bfloat16)
    segment, position = seq_layout(lengths[0], tok_rows)
    cosine, sine_part = rope_tables(position, HEAD)
    query_raw = jnp.dot(normed_one, w_query, preferred_element_type=jnp.float32).reshape(
        tok_rows, kv_local * group_size, HEAD
    )
    key_raw = jnp.dot(normed_one, w_key, preferred_element_type=jnp.float32).reshape(
        tok_rows, kv_local, HEAD
    )
    value_low = (
        jnp.dot(normed_one, w_value, preferred_element_type=jnp.float32)
        .astype(jnp.bfloat16)
        .reshape(tok_rows, kv_local, HEAD)
    )
    query_rot = (
        rotate(query_raw, cosine, sine_part)
        .astype(jnp.bfloat16)
        .reshape(tok_rows, kv_local, group_size, HEAD)
    )
    key_rot = rotate(key_raw, cosine, sine_part).astype(jnp.bfloat16)
    key_place = jnp.arange(tok_rows, dtype=jnp.int32)

    def block_scores(block_index):
        first_row = block_index * block_rows
        row_place = first_row + jnp.arange(block_rows, dtype=jnp.int32)
        allowed = (segment[:, None] == segment[None, :]) & (
            key_place[None, :] <= row_place[:, None]
        )
        scores = (
            jnp.einsum("bkgh,nkh->kgbn", query_rot, key_rot, preferred_element_type=jnp.float32)
            * score_scale
        )
        return (query_rot, jnp.where(allowed, scores, -1e30))

    def forward_block(block_index):
        unused, scores = block_scores(block_index)
        row_max = jnp.max(scores, axis=-1, keepdims=True)
        exp_terms = jnp.exp(scores - row_max)
        row_total = jnp.sum(exp_terms, axis=-1, keepdims=True)
        prob_low = (exp_terms / row_total).astype(jnp.bfloat16)
        mixed_out = jnp.einsum(
            "kgbn,nkh->bkgh", prob_low, value_low, preferred_element_type=jnp.float32
        )
        return (mixed_out.astype(jnp.bfloat16), (row_max + jnp.log(row_total))[..., 0])

    attended, log_total = lax.map(forward_block, jnp.arange(block_count, dtype=jnp.int32))
    attended_flat = attended.reshape(tok_rows, kv_local * group_size * HEAD)
    attn_partial = jnp.dot(attended_flat, w_out, preferred_element_type=jnp.float32)
    residual = x_full + lax.psum(attn_partial, "tp")
    gate_weights, up_weights, down_weights = (expert_gate, expert_up, expert_down)
    scale_two = lax.rsqrt(jnp.mean(residual * residual, axis=1, keepdims=True) + EPSILON)
    normed_two = (residual * scale_two * norm_moe).astype(jnp.bfloat16)
    logits = jnp.dot(normed_two, router, preferred_element_type=jnp.float32)
    chosen = jnp.take_along_axis(logits, expert_ids, axis=1)
    chosen_exp = jnp.exp(chosen - jnp.max(chosen, axis=1, keepdims=True))
    gates = chosen_exp / jnp.sum(chosen_exp, axis=1, keepdims=True)
    pair_slot, slot_owner = slot_table(expert_ids, EXPERTS, CAP)
    owner_token = slot_owner // TOP
    padded_two = jnp.concatenate([normed_two, jnp.zeros((1, model_width), jnp.bfloat16)], axis=0)
    expert_rows = to_experts(padded_two, owner_token, None)
    gate_pre = jnp.einsum(
        "erd,edf->erf", expert_rows, gate_weights, preferred_element_type=jnp.float32
    )
    up_pre = jnp.einsum("erd,edf->erf", expert_rows, up_weights, preferred_element_type=jnp.float32)
    gate_sig = jax.nn.sigmoid(gate_pre)
    active = (gate_pre * gate_sig * up_pre).astype(jnp.bfloat16)
    down_partial = jnp.einsum(
        "erf,efd->erd", active, down_weights, preferred_element_type=jnp.float32
    )
    returned = to_sources(down_partial)
    per_pair = returned.reshape(EXPERTS * CAP, model_width)[pair_slot].reshape(
        tok_rows, TOP, model_width
    )
    mixture = jnp.sum(gates[:, :, None] * per_pair.astype(jnp.float32), axis=1)
    output = (residual + mixture).astype(jnp.bfloat16)
    grad_out = out_grad.astype(jnp.float32)
    grad_gates = jnp.sum(grad_out[:, None, :] * per_pair.astype(jnp.float32), axis=2)
    grad_chosen = gates * (grad_gates - jnp.sum(gates * grad_gates, axis=1, keepdims=True))
    expert_columns = jnp.arange(EXPERTS, dtype=jnp.int32)
    grad_logits = jnp.sum(
        grad_chosen[:, :, None]
        * (expert_ids[:, :, None] == expert_columns[None, None, :]).astype(jnp.float32),
        axis=1,
    )
    grad_router = jnp.dot(normed_two.astype(jnp.float32).T, grad_logits, precision=highest)
    router_input = jnp.dot(grad_logits, router.astype(jnp.float32).T, precision=highest)
    gates_padded = jnp.concatenate([gates.reshape(-1), jnp.zeros((1,), jnp.float32)])
    slot_gate = gates_padded[slot_owner]
    grad_padded = jnp.concatenate([grad_out, jnp.zeros((1, model_width), jnp.float32)], axis=0)
    grad_rows = to_experts(grad_padded, owner_token, slot_gate)
    grad_active = jnp.einsum(
        "erd,efd->erf", grad_rows, down_weights, preferred_element_type=jnp.float32
    )
    grad_gate_pre = (grad_active * up_pre * gate_sig * (1.0 + gate_pre * (1.0 - gate_sig))).astype(
        jnp.bfloat16
    )
    grad_up_pre = (grad_active * gate_pre * gate_sig).astype(jnp.bfloat16)
    grad_expert_down = jnp.einsum(
        "erf,erd->efd", active, grad_rows, preferred_element_type=jnp.float32
    )
    grad_expert_gate = jnp.einsum(
        "erd,erf->edf", expert_rows, grad_gate_pre, preferred_element_type=jnp.float32
    )
    grad_expert_up = jnp.einsum(
        "erd,erf->edf", expert_rows, grad_up_pre, preferred_element_type=jnp.float32
    )
    row_partial = jnp.einsum(
        "erf,edf->erd", grad_gate_pre, gate_weights, preferred_element_type=jnp.float32
    )
    row_partial = row_partial + jnp.einsum(
        "erf,edf->erd", grad_up_pre, up_weights, preferred_element_type=jnp.float32
    )
    row_back = to_sources(row_partial)
    grad_pairs = row_back.reshape(EXPERTS * CAP, model_width)[pair_slot].reshape(
        tok_rows, TOP, model_width
    )
    grad_normed_two = jnp.sum(grad_pairs.astype(jnp.float32), axis=1) + router_input
    weighted_two = grad_normed_two * norm_moe
    grad_norm_moe = jnp.sum(grad_normed_two * residual * scale_two, axis=0)
    grad_residual = (
        grad_out
        + scale_two * weighted_two
        - residual * scale_two**3 * jnp.mean(weighted_two * residual, axis=1, keepdims=True)
    )
    grad_attn = grad_residual.astype(jnp.bfloat16)
    grad_w_out = jnp.dot(attended_flat.T, grad_attn, preferred_element_type=jnp.float32)
    grad_attended = (
        jnp.dot(grad_attn, w_out.T, preferred_element_type=jnp.float32)
        .astype(jnp.bfloat16)
        .reshape(tok_rows, kv_local, group_size, HEAD)
    )

    def backward_block(carried, block_index):
        grad_key, grad_value = carried
        first_row = block_index * block_rows
        query_block, scores = block_scores(block_index)
        prob_full = jnp.exp(scores - log_total[block_index][..., None])
        prob_low = prob_full.astype(jnp.bfloat16)
        grad_prob = jnp.einsum(
            "bkgh,nkh->kgbn", grad_attended, value_low, preferred_element_type=jnp.float32
        )
        row_inner = jnp.sum(prob_full * grad_prob, axis=-1, keepdims=True)
        grad_scores = (prob_full * (grad_prob - row_inner)).astype(jnp.bfloat16)
        grad_query_block = (
            jnp.einsum("kgbn,nkh->bkgh", grad_scores, key_rot, preferred_element_type=jnp.float32)
            * score_scale
        )
        grad_key = (
            grad_key
            + jnp.einsum(
                "kgbn,bkgh->nkh", grad_scores, query_block, preferred_element_type=jnp.float32
            )
            * score_scale
        )
        grad_value = grad_value + jnp.einsum(
            "kgbn,bkgh->nkh", prob_low, grad_attended, preferred_element_type=jnp.float32
        )
        return ((grad_key, grad_value), grad_query_block)

    zero_heads = jnp.zeros((tok_rows, kv_local, HEAD), jnp.float32)
    (grad_key, grad_value), grad_query = lax.scan(
        backward_block, (zero_heads, zero_heads), jnp.arange(block_count, dtype=jnp.int32)
    )
    grad_query_low = (
        unrotate(grad_query.reshape(tok_rows, kv_local * group_size, HEAD), cosine, sine_part)
        .astype(jnp.bfloat16)
        .reshape(tok_rows, kv_local * group_size * HEAD)
    )
    grad_key_low = (
        unrotate(grad_key, cosine, sine_part)
        .astype(jnp.bfloat16)
        .reshape(tok_rows, kv_local * HEAD)
    )
    grad_value_low = grad_value.astype(jnp.bfloat16).reshape(tok_rows, kv_local * HEAD)
    grad_w_query = jnp.dot(normed_one.T, grad_query_low, preferred_element_type=jnp.float32)
    grad_w_key = jnp.dot(normed_one.T, grad_key_low, preferred_element_type=jnp.float32)
    grad_w_value = jnp.dot(normed_one.T, grad_value_low, preferred_element_type=jnp.float32)
    input_partial = jnp.dot(grad_query_low, w_query.T, preferred_element_type=jnp.float32)
    input_partial = input_partial + jnp.dot(
        grad_key_low, w_key.T, preferred_element_type=jnp.float32
    )
    input_partial = input_partial + jnp.dot(
        grad_value_low, w_value.T, preferred_element_type=jnp.float32
    )
    grad_normed_one = lax.psum(input_partial.astype(jnp.bfloat16), "tp").astype(jnp.float32)
    weighted_one = grad_normed_one * norm_attn
    grad_norm_attn = jnp.sum(grad_normed_one * x_full * scale_one, axis=0)
    grad_tokens = (
        grad_residual
        + scale_one * weighted_one
        - x_full * scale_one**3 * jnp.mean(weighted_one * x_full, axis=1, keepdims=True)
    )
    summed = (
        lax.psum(grad_norm_attn.astype(jnp.bfloat16), "ep").astype(jnp.float32),
        lax.psum(grad_w_query.astype(jnp.bfloat16), "ep").astype(jnp.float32),
        lax.psum(grad_w_key.astype(jnp.bfloat16), "ep").astype(jnp.float32),
        lax.psum(grad_w_value.astype(jnp.bfloat16), "ep").astype(jnp.float32),
        lax.psum(grad_w_out.astype(jnp.bfloat16), "ep").astype(jnp.float32),
        lax.psum(grad_norm_moe.astype(jnp.bfloat16), "ep").astype(jnp.float32),
        lax.psum(grad_router.astype(jnp.bfloat16), "ep").astype(jnp.float32),
    )
    return (
        output,
        grad_tokens.astype(jnp.bfloat16),
        summed[0],
        summed[1],
        summed[2],
        summed[3],
        summed[4],
        summed[5],
        summed[6],
        grad_expert_gate,
        grad_expert_up,
        grad_expert_down,
    )


def solution(mesh):
    in_specs = (
        P("ep", None),
        P(),
        P(None, "tp"),
        P(None, "tp"),
        P(None, "tp"),
        P("tp", None),
        P(),
        P(),
        P("ep", None, "tp"),
        P("ep", None, "tp"),
        P("ep", "tp", None),
        P("ep", None),
        P("ep", None),
        P("ep", None),
    )
    out_specs = (
        P("ep", None),
        P("ep", None),
        P(),
        P(None, "tp"),
        P(None, "tp"),
        P(None, "tp"),
        P("tp", None),
        P(),
        P(),
        P("ep", None, "tp"),
        P("ep", None, "tp"),
        P("ep", "tp", None),
    )
    return jax.shard_map(body, mesh=mesh, in_specs=in_specs, out_specs=out_specs, check_vma=False)
```

profile of v0, /device:TPU:0, one launch (start us, length us, event | category | flops | bytes accessed | tf_op | source)
XLA Modules:
  0.0 1778.4 jit_solution(8088556260049350305)
XLA Ops:
  23.0 9.2 reduce-window.11
  33.9 15.5 scatter_custom_fusion
  50.1 26.4 %all-reduce.8.cloned.1.call-done = f32[512,1024]{1,0:T(8,128)} async-done(((f32[512,1024]{1,0:T(8,128)}), f32[512,1024]{1,0:T(8,128)}) %all-reduce.8.cloned.1.call-update) | async-done | bytes 2097168 | tf_op jit(solution)/shard_map/psum | solution.py:156
  80.4 26.8 %gather_fusion = bf16[6144,1024]{1,0:T(8,128)(2,1)} fusion(bf16[513,1024]{1,0:T(8,128)(2,1)S(1)} %concatenate.44, s32[6144]{0:T(1024)S(1)} %get-tuple-element.102), kind=kCustom, calls=%fused_computation | custom fusion | bytes 25190400 | tf_op jit(solution)/shard_map/gather | solution.py:68
  114.8 27.6 %gather_fusion.3 = f32[6144,1024]{1,0:T(8,128)} fusion(f32[513,1024]{1,0:T(8,128)S(1)} %concatenate.46, s32[6144]{0:T(1024)S(1)} %get-tuple-element.102), kind=kCustom, calls=%fused_computation.3 | custom fusion | bytes 50356224 | tf_op jit(solution)/shard_map/gather | solution.py:68
  144.0 33.0 %gather_fusion.5 = f32[4096]{0:T(1024)S(1)} fusion(f32[512,32]{0,1:T(8,128)S(1)} %fusion.68, s32[4096]{0:T(1024)S(1)} %reshape.397), kind=kCustom, calls=%fused_computation.5 | custom fusion | bytes 65536 | tf_op jit(solution)/shard_map/jit(take_along_axis)/gather | solution.py:161
  178.4 34.3 %gather_fusion.2 = f32[6144]{0:T(1024)S(1)} fusion(f32[4097]{0:T(1024)S(1)} %pad_maximum_fusion.2, s32[6144]{0:T(1024)S(1)} %copy-done.52), kind=kCustom, calls=%fused_computation.2 | custom fusion | bytes 73728 | tf_op jit(solution)/shard_map/gather | solution.py:195
  212.8 13.3 multiply_convert_fusion
  226.1 159.8 %all-to-all-done = bf16[32,192,1024]{2,1,0:T(8,128)(2,1)} async-done(((bf16[32,192,1024]{2,1,0:T(8,128)(2,1)}), bf16[32,192,1024]{2,1,0:T(8,128)(2,1)}, u32[]{:S(2)}, u32[]{:S(2)}) %all-to-all-start) | async-done | bytes 12582944 | tf_op jit(solution)/shard_map/all_to_all | solution.py:72
  408.4 254.8 %all-to-all-done.2 = bf16[32,192,1024]{2,1,0:T(8,128)(2,1)} async-done(((bf16[32,192,1024]{2,1,0:T(8,128)(2,1)}), bf16[32,192,1024]{2,1,0:T(8,128)(2,1)}, u32[]{:S(2)}, u32[]{:S(2)}) %all-to-all-start.2) | async-done | bytes 12582944 | tf_op jit(solution)/shard_map/all_to_all | solution.py:72
  663.3 11.0 copy.133
  674.3 11.4 multiply_convert_fusion.1
  685.8 10.3 fusion.72
  696.1 20.7 %convolution_add_fusion = f32[4,1536,1024]{2,1,0:T(8,128)} fusion(f32[4,1536,1024]{2,1,0:T(8,128)} %fusion.72, bf16[4,1536,128]{2,1,0:T(8,128)(2,1)} %get-tuple-element.84, bf16[4,1024,128]{2,1,0:T(8,128)(2,1)} %param.23), kind=kOutput, calls=%fused_computation.10 | convolution fusion | flops 1616904192 | bytes 52953088 | tf_op jit(solution)/shard_map/erf,edf->erd/dot_general | solution.py:217
  716.9 179.0 %reduce-scatter.5.cloned.1.call-done = f32[4,1536,256]{2,1,0:T(8,128)} async-done(((f32[4,1536,1024]{2,1,0:T(8,128)}), f32[4,1536,256]{2,1,0:T(8,128)}) %reduce-scatter.5.cloned.1.call-update) | async-done | bytes 6291472 | tf_op jit(solution)/shard_map/reduce_scatter | solution.py:76
  900.7 12.7 fusion.71
  913.4 71.1 %all-gather.5.cloned.1.call-done = bf16[4,1536,1024]{2,1,0:T(8,128)(2,1)} async-done(((bf16[4,1536,256]{2,1,0:T(8,128)(2,1)}), bf16[4,1536,1024]{2,1,0:T(8,128)(2,1)}) %all-gather.5.cloned.1.call-update) | async-done | bytes 12582928 | tf_op jit(solution)/shard_map/all_gather | solution.py:79
  984.6 17.2 copy.134
  1007.5 159.9 %reduce-scatter.3.cloned.1.call-done = f32[4,1536,256]{2,1,0:T(8,128)} async-done(((f32[4,1536,1024]{2,1,0:T(8,128)}), f32[4,1536,256]{2,1,0:T(8,128)}) %reduce-scatter.3.cloned.1.call-update) | async-done | bytes 6291472 | tf_op jit(solution)/shard_map/reduce_scatter | solution.py:76
  1172.2 83.9 %all-gather.3.cloned.1.call-done = bf16[4,1536,1024]{2,1,0:T(8,128)(2,1)} async-done(((bf16[4,1536,256]{2,1,0:T(8,128)(2,1)}), bf16[4,1536,1024]{2,1,0:T(8,128)(2,1)}) %all-gather.3.cloned.1.call-update) | async-done | bytes 12582928 | tf_op jit(solution)/shard_map/all_gather | solution.py:79
  1256.2 17.2 copy.130
  1289.2 10.7 fusion.76
  1308.6 13.1 copy.135
  1321.7 27.2 %gather_fusion.4 = bf16[4096,1024]{1,0:T(8,128)(2,1)} fusion(bf16[6144,1024]{1,0:T(8,128)(2,1)} %bitcast.167, s32[4096]{0:T(1024)S(1)} %broadcast_clamp_fusion), kind=kCustom, calls=%fused_computation.4 | custom fusion | bytes 16793600 | tf_op jit(solution)/shard_map/gather | solution.py:221
  1348.9 11.9 convert_reduce_fusion
  1360.8 198.5 %all-to-all-done.1 = bf16[4,1536,1024]{2,0,1:T(4,128)(2,1)} async-done(((bf16[4,1536,1024]{2,0,1:T(4,128)(2,1)}), bf16[4,1536,1024]{2,0,1:T(4,128)(2,1)}, u32[]{:S(2)}, u32[]{:S(2)}) %all-to-all-start.1) | async-done | bytes 12582944 | tf_op jit(solution)/shard_map/all_to_all | solution.py:80
  1559.3 13.1 copy.131
  1572.5 27.2 %gather_fusion.1 = bf16[4096,1024]{1,0:T(8,128)(2,1)} fusion(bf16[6144,1024]{1,0:T(8,128)(2,1)} %bitcast.166, s32[4096]{0:T(1024)S(1)} %broadcast_clamp_fusion), kind=kCustom, calls=%fused_computation.1 | custom fusion | bytes 16793600 | tf_op jit(solution)/shard_map/gather | solution.py:178
  1599.7 10.6 fusion.1
  1643.3 21.8 %all-reduce.10.cloned.1.call-done = bf16[512,1024]{1,0:T(8,128)(2,1)} async-done(((bf16[512,1024]{1,0:T(8,128)(2,1)}), bf16[512,1024]{1,0:T(8,128)(2,1)}) %all-reduce.10.cloned.1.call-update) | async-done | bytes 1048592 | tf_op jit(solution)/shard_map/psum | solution.py:292
  1667.5 21.9 %all-reduce.2 = (bf16[1024]{0:T(1024)(128)(2,1)S(1)}, bf16[1024]{0:T(1024)(128)(2,1)S(1)}) all-reduce(bf16[1024]{0:T(1024)(128)(2,1)S(1)} %get-tuple-element.62, bf16[1024]{0:T(1024)(128)(2,1)S(1)} %get-tuple-element.60), channel_id=1, replica_groups=mesh['ep'=8,'tp'=4] {'ep'}, use_global_device_ids=true, to_apply=%region_26.27 | all-reduce | flops 2048 | bytes 8192 | tf_op jit(solution)/shard_map/psum | solution.py:301
  1693.8 69.9 %all-reduce.12.cloned.1.call-done = (bf16[1024,256]{1,0:T(8,128)(2,1)}, bf16[1024,128]{1,0:T(8,128)(2,1)}, bf16[1024,128]{1,0:T(8,128)(2,1)}, bf16[256,1024]{1,0:T(8,128)(2,1)}, bf16[1024,32]{0,1:T(8,128)(2,1)}) async-done(((bf16[1024,256]{1,0:T(8,128)(2,1)}, bf16[1024,128]{1,0:T(8,128)(2,1)}, bf16[1024,128]{1,0:T(8,128)(2,1)}, bf16[256,1024]{1,0:T(8,128)(2,1)}, bf16[1024,32]{0,1:T(8,128)(2,1)}), ...) | async-done | bytes 1638416 | tf_op jit(solution)/shard_map/psum | solution.py:302
  (260 shorter events, 141.4 us)
Async XLA Ops:
  7.2 667.1 %copy-start = (bf16[4,128,1024]{2,1,0:T(8,128)(2,1)S(1)}, bf16[4,128,1024]{2,1,0:T(8,128)(2,1)}, u32[]{:S(2)}) copy-start(bf16[4,128,1024]{2,1,0:T(8,128)(2,1)} %param.24) | copy-start | bytes 3145732
  7.2 6.1 copy-start.7
  7.2 69.3 %all-reduce.8.cloned.1.call-start = ((), (), s32[]{:S(2)}) async-start(), calls=%async_computation.6 | async-start | bytes 4194304 | tf_op jit(solution)/shard_map/psum | solution.py:156
  33.8 44.6 %copy-start.53 = (s32[4096,1]{0,1:T(1,128)}, s32[4096,1]{0,1:T(1,128)S(1)}, u32[]{:S(2)}) copy-start(s32[4096,1]{0,1:T(1,128)S(1)} %compare_select_fusion) | copy-start | bytes 49156
  50.1 29.0 %copy-start.55 = (f32[1024]{0:T(1024)S(1)}, f32[1024]{0:T(1024)}, u32[]{:S(2)}) copy-start(f32[1024]{0:T(1024)} %param.20) | copy-start | bytes 12292
  107.2 278.7 %all-to-all-start = ((bf16[32,192,1024]{2,1,0:T(8,128)(2,1)}), bf16[32,192,1024]{2,1,0:T(8,128)(2,1)}, u32[]{:S(2)}, u32[]{:S(2)}) async-start(bf16[32,192,1024]{2,1,0:T(8,128)(2,1)} %bitcast.171), calls=%async_computation | async-start | bytes 25165824 | tf_op jit(solution)/shard_map/all_to_all | solution.py:72
  114.8 27.6 %copy-start.41 = (bf16[1024,32]{0,1:T(8,128)(2,1)S(1)}, bf16[1024,32]{0,1:T(8,128)(2,1)}, u32[]{:S(2)}) copy-start(bf16[1024,32]{0,1:T(8,128)(2,1)} %param.21) | copy-start | bytes 196612
  144.0 34.4 %copy-start.52 = (s32[6144]{0:T(1024)S(1)}, s32[6144]{0:T(1024)}, u32[]{:S(2)}) copy-start(s32[6144]{0:T(1024)} %get-tuple-element.101) | copy-start | bytes 73732
  177.4 35.3 %copy-start.47 = (f32[512,8]{0,1:T(8,128)}, f32[512,8]{0,1:T(8,128)S(1)}, u32[]{:S(2)}) copy-start(f32[512,8]{0,1:T(8,128)S(1)} %fusion.50) | copy-start | bytes 49156
  385.9 277.4 %all-to-all-start.2 = ((bf16[32,192,1024]{2,1,0:T(8,128)(2,1)}), bf16[32,192,1024]{2,1,0:T(8,128)(2,1)}, u32[]{:S(2)}, u32[]{:S(2)}) async-start(bf16[32,192,1024]{2,1,0:T(8,128)(2,1)} %multiply_convert_fusion), calls=%async_computation.3 | async-start | bytes 25165824 | tf_op jit(solution)/shard_map/all_to_all | solution.py:72
  391.3 504.6 %reduce-scatter.5.cloned.1.call-start = ((), (), s32[]{:S(2)}) async-start(), calls=%async_computation.9 | async-start | bytes 31457280 | tf_op jit(solution)/shard_map/reduce_scatter | solution.py:76
  391.3 6.5 copy-start.17
  663.3 11.0 copy-start.69
  674.3 11.4 copy-start.32
  685.8 10.3 copy-start.24
  685.8 214.9 %copy-start.14 = (bf16[4,1536,128]{2,1,0:T(8,128)(2,1)}, bf16[4,1536,128]{2,1,0:T(8,128)(2,1)S(1)}, u32[]{:S(2)}) copy-start(bf16[4,1536,128]{2,1,0:T(8,128)(2,1)S(1)} %get-tuple-element.86) | copy-start | bytes 4718596
  716.8 267.7 %all-gather.5.cloned.1.call-start = ((), (), s32[]{:S(2)}) async-start(), calls=%async_computation.10 | async-start | bytes 15728640 | tf_op jit(solution)/shard_map/all_gather | solution.py:79
  900.6 266.9 %reduce-scatter.3.cloned.1.call-start = ((), (), s32[]{:S(2)}) async-start(), calls=%async_computation.7 | async-start | bytes 31457280 | tf_op jit(solution)/shard_map/reduce_scatter | solution.py:76
  1001.8 279.4 %all-to-all-start.3 = ((bf16[4,1536,1024]{2,0,1:T(4,128)(2,1)}), bf16[4,1536,1024]{2,0,1:T(4,128)(2,1)}, u32[]{:S(2)}, u32[]{:S(2)}) async-start(bf16[4,1536,1024]{2,0,1:T(4,128)(2,1)} %copy.134), calls=%async_computation.5 | async-start | bytes 25165824 | tf_op jit(solution)/shard_map/all_to_all | solution.py:80
  1007.5 248.7 %all-gather.3.cloned.1.call-start = ((), (), s32[]{:S(2)}) async-start(), calls=%async_computation.8 | async-start | bytes 15728640 | tf_op jit(solution)/shard_map/all_gather | solution.py:79
  1273.3 13.7 copy-start.11
  1281.1 278.2 %all-to-all-start.1 = ((bf16[4,1536,1024]{2,0,1:T(4,128)(2,1)}), bf16[4,1536,1024]{2,0,1:T(4,128)(2,1)}, u32[]{:S(2)}, u32[]{:S(2)}) async-start(bf16[4,1536,1024]{2,0,1:T(4,128)(2,1)} %copy.130), calls=%async_computation.2 | async-start | bytes 25165824 | tf_op jit(solution)/shard_map/all_to_all | solution.py:80
  1286.5 378.6 %all-reduce.10.cloned.1.call-start = ((), (), s32[]{:S(2)}) async-start(), calls=%async_computation.11 | async-start | bytes 2097152 | tf_op jit(solution)/shard_map/psum | solution.py:292
  1289.2 10.7 copy-start.25
  1572.5 27.2 %copy-start.16 = (f32[512,8]{1,0:T(8,128)S(1)}, f32[512,8]{1,0:T(8,128)}, u32[]{:S(2)}) copy-start(f32[512,8]{1,0:T(8,128)} %copy-done.15) | copy-start | bytes 49156
  1599.6 11.7 copy-start.48
  1599.6 11.7 copy-start.34
  1599.6 11.8 copy-start.4
  1599.6 11.8 copy-start.42
  1630.8 133.0 %all-reduce.12.cloned.1.call-start = ((), (), s32[]{:S(2)}) async-start(), calls=%async_computation.12 | async-start | bytes 3276800 | tf_op jit(solution)/shard_map/psum | solution.py:302
  1643.3 47.3 %copy-start.67 = (f32[512]{0:T(512)S(1)}, f32[512]{0:T(512)}, u32[]{:S(2)}) copy-start(f32[512]{0:T(512)} %get-tuple-element.103) | copy-start | bytes 6148
  1763.8 6.3 copy-start.37
  (49 other events, 113.3 us)
Sparse Core Ops, SparseCore 0:
  22.3 54.1 all-reduce.7
  716.9 178.8 reduce-scatter.4
  900.7 83.7 all-gather.4
  987.0 180.4 reduce-scatter.2
  1172.3 83.7 all-gather.2
  1630.9 34.1 all-reduce.9
  1670.4 93.3 all-reduce.11
where the time goes:
time: 1790 us; the launch traced here: 1780 us
  waiting for transfers between devices  1230 us (69%)
  local copies, waits for them, and re-layouts  281 us (16%)
  matrix products  119 us (7%)
  other arithmetic  84.6 us (5%)
  starting transfers between devices  23.1 us (1%)
  blocking collectives  21.9 us (1%)
    all_to_all x2, waiting for transfers between devices, to_experts(): return lax.all_to_all(buffer, 'ep', split_axis=0, concat_axis=1, tiled=True)  415 us
    reduce_scatter x2, waiting for transfers between devices, to_sources(): lax.psum_scatter(partial_rows, 'tp', scatter_dimension=2, tiled=True)  339 us
    all_to_all x2, waiting for transfers between devices, to_sources(): return lax.all_to_all(joined, 'ep', split_axis=1, concat_axis=0, tiled=True)  206 us
    all_gather x2, waiting for transfers between devices, to_sources(): joined = lax.all_gather(summed, 'tp', axis=2, tiled=True)  155 us
    psum x1, waiting for transfers between devices, body(): lax.psum(grad_w_query.astype(jnp.bfloat16), 'ep').astype(jnp.float32)  69.9 us
    gather x2, local copies, waits for them, and re-layouts, to_experts(): picked = padded_rows[owner_token]  54.4 us
  transfers between devices with their start and end apart: 11, of which 11 were waited for; matrix products, arithmetic and copies ran while one was open for 17% of the time, Pallas kernels for 0%

commit v1 on v0

v1 whole, which is shorter than its diff:
```python
import jax
import jax.numpy as jnp
import numpy as np
from jax import lax
from jax.sharding import PartitionSpec as P

HEAD = 64
EPSILON = 1e-06
ROPE_BASE = 10000.0
BOTH = ("ep", "tp")
BF = jnp.bfloat16
F32 = jnp.float32


def mm(a, b):
    return jnp.dot(a, b, preferred_element_type=F32)


def mm_nt(a, b):
    return lax.dot_general(a, b, (((1,), (1,)), ((), ())), preferred_element_type=F32)


def mm_tn(a, b):
    return lax.dot_general(a, b, (((0,), (0,)), ((), ())), preferred_element_type=F32)


def seq_layout(seq_lengths, tok_rows):
    seq_ends = jnp.cumsum(seq_lengths, dtype=jnp.int32)
    seq_starts = seq_ends - seq_lengths
    places = jnp.arange(tok_rows, dtype=jnp.int32)
    segment = jnp.sum(
        (places[:, None] >= seq_ends[None, :]).astype(jnp.int32), axis=1, dtype=jnp.int32
    )
    slot_match = segment[:, None] == jnp.arange(seq_lengths.shape[0], dtype=jnp.int32)[None, :]
    begins = jnp.sum(jnp.where(slot_match, seq_starts[None, :], 0), axis=1, dtype=jnp.int32)
    return (segment, places - begins)


def turn_columns(weights):
    rows, columns = weights.shape
    split = weights.reshape(rows, columns // HEAD, 2, HEAD // 2)
    return jnp.stack([-split[:, :, 1], split[:, :, 0]], axis=2).reshape(rows, columns)


def turn_matrix(columns):
    half = HEAD // 2
    turn = np.zeros((columns, columns), np.float32)
    for first in range(0, columns, HEAD):
        for i in range(half):
            turn[first + half + i, first + i] = 1.0
            turn[first + i, first + half + i] = -1.0
    return jnp.asarray(turn, BF)


def body(
    tokens,
    norm_attn,
    w_query,
    w_key,
    w_value,
    w_out,
    norm_moe,
    router,
    expert_gate,
    expert_up,
    expert_down,
    lengths,
    expert_ids,
    out_grad,
):
    highest = lax.Precision.HIGHEST
    tok_rows, width = tokens.shape
    q_cols, k_cols = w_query.shape[1], w_key.shape[1]
    kv = k_cols // HEAD
    group = q_cols // k_cols
    tp_size = lax.axis_size("tp")
    tp_at = lax.axis_index("tp")
    ep_at = lax.axis_index("ep")
    own = tok_rows // tp_size
    local_experts, _, ff = expert_gate.shape
    experts = router.shape[1]
    first = tp_at * own
    score_scale = HEAD ** (-0.5)

    def mine(array):
        return lax.dynamic_slice_in_dim(array, first, own, 0)

    grad_own = mine(out_grad)
    grad_all = lax.all_gather(grad_own, BOTH, axis=0, tiled=True)
    ids_own = mine(expert_ids)
    mask_own = jnp.sum(
        (ids_own[:, :, None] == jnp.arange(experts, dtype=jnp.int32)[None, None, :]).astype(F32),
        axis=1,
    )
    mask_all = lax.all_gather(mask_own.astype(BF), BOTH, axis=0, tiled=True)

    w_gate_up = jnp.concatenate(
        [
            jnp.transpose(expert_gate, (1, 0, 2)).reshape(width, local_experts * ff),
            jnp.transpose(expert_up, (1, 0, 2)).reshape(width, local_experts * ff),
        ],
        axis=1,
    )
    w_down = expert_down.reshape(local_experts * ff, width)

    x_full = tokens.astype(F32)
    scale_one = lax.rsqrt(jnp.mean(x_full * x_full, axis=1, keepdims=True) + EPSILON)
    normed_one = (x_full * scale_one * norm_attn).astype(BF)
    segment, position = seq_layout(lengths[0], tok_rows)
    half = HEAD // 2
    inverse = ROPE_BASE ** (-2.0 * jnp.arange(half, dtype=F32) / HEAD)
    angles = position.astype(F32)[:, None] * inverse[None, :]
    cos_half, sin_half = jnp.cos(angles), jnp.sin(angles)
    cosine = jnp.concatenate([cos_half, cos_half] * (q_cols // HEAD), axis=1)
    sine = jnp.concatenate([sin_half, sin_half] * (q_cols // HEAD), axis=1)
    w_all = jnp.concatenate(
        [w_query, turn_columns(w_query), w_key, turn_columns(w_key), w_value], axis=1
    )
    projected = mm(normed_one, w_all)
    at = 2 * q_cols
    query_low = (projected[:, :q_cols] * cosine + projected[:, q_cols:at] * sine).astype(BF)
    key_low = (
        projected[:, at : at + k_cols] * cosine[:, :k_cols]
        + projected[:, at + k_cols : at + 2 * k_cols] * sine[:, :k_cols]
    ).astype(BF)
    value_flat = projected[:, at + 2 * k_cols :].astype(BF)

    def heads_q(array):
        return (
            array.reshape(tok_rows, kv, group, HEAD)
            .transpose(1, 2, 0, 3)
            .reshape(kv, group * tok_rows, HEAD)
        )

    def flat_q(array):
        return (
            array.reshape(kv, group, tok_rows, HEAD)
            .transpose(2, 0, 1, 3)
            .reshape(tok_rows, q_cols)
        )

    def heads_k(array):
        return array.reshape(tok_rows, kv, HEAD).transpose(1, 0, 2)

    def flat_k(array):
        return array.transpose(1, 0, 2).reshape(tok_rows, k_cols)

    query, key, value = heads_q(query_low), heads_k(key_low), heads_k(value_flat)
    place = jnp.arange(tok_rows, dtype=jnp.int32)
    allowed = (segment[:, None] == segment[None, :]) & (place[None, :] <= place[:, None])
    allowed = jnp.concatenate([allowed] * group, axis=0)
    scores = jnp.einsum("kbh,knh->kbn", query, key, preferred_element_type=F32) * score_scale
    scores = jnp.where(allowed[None], scores, -1e30)
    row_max = jnp.max(scores, axis=-1, keepdims=True)
    exp_terms = jnp.exp(scores - row_max)
    probs_full = exp_terms / jnp.sum(exp_terms, axis=-1, keepdims=True)
    prob_low = probs_full.astype(BF)
    mixed = jnp.einsum("kbn,knh->kbh", prob_low, value, preferred_element_type=F32)
    attended = flat_q(mixed.astype(BF))
    attn_partial = mm(attended, w_out)
    x_own = mine(tokens).astype(F32)
    residual = x_own + lax.psum_scatter(attn_partial, "tp", scatter_dimension=0, tiled=True)
    scale_two = lax.rsqrt(jnp.mean(residual * residual, axis=1, keepdims=True) + EPSILON)
    normed_two = (residual * scale_two * norm_moe).astype(BF)

    rows_all = lax.all_gather(normed_two, BOTH, axis=0, tiled=True)
    logits = mm(rows_all, router)
    mask = mask_all > 0
    masked = jnp.where(mask, logits, -jnp.inf)
    chosen_exp = jnp.where(
        mask, jnp.exp(logits - jnp.max(masked, axis=1, keepdims=True)), 0.0
    )
    gates_all = chosen_exp / jnp.sum(chosen_exp, axis=1, keepdims=True)
    gates = lax.dynamic_slice_in_dim(gates_all, ep_at * local_experts, local_experts, 1)
    all_rows = rows_all.shape[0]
    wide = local_experts * ff
    gate_wide = jnp.concatenate(
        [jnp.broadcast_to(gates[:, e : e + 1], (all_rows, ff)) for e in range(local_experts)],
        axis=1,
    )
    pre = mm(rows_all, w_gate_up)
    gate_pre, up_pre = pre[:, :wide], pre[:, wide:]
    grad_act = mm_nt(grad_all, w_down)
    sig = jax.nn.sigmoid(gate_pre)
    active = gate_pre * sig * up_pre
    grad_gates_wide = active * grad_act
    grad_gates_part = jnp.concatenate(
        [
            jnp.sum(grad_gates_wide[:, e * ff : (e + 1) * ff], axis=1, keepdims=True)
            for e in range(local_experts)
        ],
        axis=1,
    )
    weighted = (gate_wide * active).astype(BF)
    scaled_grad = gate_wide * grad_act
    grad_pre = jnp.concatenate(
        [
            (scaled_grad * up_pre * sig * (1.0 + gate_pre * (1.0 - sig))).astype(BF),
            (scaled_grad * gate_pre * sig).astype(BF),
        ],
        axis=1,
    )
    gates_dense = lax.dynamic_update_slice_in_dim(
        jnp.zeros((all_rows, experts), F32), grad_gates_part, ep_at * local_experts, 1
    )
    grad_gates = lax.psum_scatter(gates_dense, BOTH, scatter_dimension=0, tiled=True)
    row_part = mm_nt(grad_pre, w_gate_up).astype(BF)
    row_grads = lax.psum_scatter(row_part, BOTH, scatter_dimension=0, tiled=True)
    mix_part = mm(weighted, w_down).astype(BF)
    mixture = lax.psum_scatter(mix_part, BOTH, scatter_dimension=0, tiled=True)
    grad_w_gu = mm_tn(rows_all, grad_pre)
    grad_w_gu = grad_w_gu.reshape(width, 2, local_experts, ff)
    grad_expert_gate = grad_w_gu[:, 0].transpose(1, 0, 2)
    grad_expert_up = grad_w_gu[:, 1].transpose(1, 0, 2)
    grad_expert_down = mm_tn(weighted, grad_all).reshape(local_experts, ff, width)

    output_own = (residual + mixture.astype(F32)).astype(BF)
    output = lax.all_gather(output_own, "tp", axis=0, tiled=True)
    logits_own = mm(normed_two, router)
    keep = mask_own > 0
    own_exp = jnp.where(
        keep,
        jnp.exp(logits_own - jnp.max(jnp.where(keep, logits_own, -jnp.inf), axis=1, keepdims=True)),
        0.0,
    )
    gates_own = own_exp / jnp.sum(own_exp, axis=1, keepdims=True)
    grad_logits = gates_own * (
        grad_gates - jnp.sum(gates_own * grad_gates, axis=1, keepdims=True)
    )
    grad_router_part = jnp.dot(grad_logits.T, normed_two.astype(F32), precision=highest)
    router_input = jnp.dot(grad_logits, router.astype(F32).T, precision=highest)
    grad_normed_two = row_grads.astype(F32) + router_input
    weighted_two = grad_normed_two * norm_moe
    grad_norm_moe = jnp.sum(grad_normed_two * residual * scale_two, axis=0)
    grad_residual = (
        grad_own.astype(F32)
        + scale_two * weighted_two
        - residual * scale_two**3 * jnp.mean(weighted_two * residual, axis=1, keepdims=True)
    )
    grad_attn = lax.all_gather(grad_residual.astype(BF), "tp", axis=0, tiled=True)
    grad_w_out = mm_tn(attended, grad_attn)

    grad_attended = heads_q(mm_nt(grad_attn, w_out).astype(BF))
    grad_prob = jnp.einsum("kbh,knh->kbn", grad_attended, value, preferred_element_type=F32)
    row_inner = jnp.sum(probs_full * grad_prob, axis=-1, keepdims=True)
    grad_scores = (probs_full * (grad_prob - row_inner)).astype(BF)
    grad_q = flat_q(jnp.einsum("kbn,knh->kbh", grad_scores, key, preferred_element_type=F32))
    grad_k = flat_k(jnp.einsum("kbn,kbh->knh", grad_scores, query, preferred_element_type=F32))
    grad_v = flat_k(jnp.einsum("kbn,kbh->knh", prob_low, grad_attended, preferred_element_type=F32))
    grad_q = grad_q * score_scale
    grad_k = grad_k * score_scale
    turn = turn_matrix(q_cols)
    grad_q_low = (grad_q * cosine + mm((grad_q * sine).astype(BF), turn)).astype(BF)
    grad_k_low = (
        grad_k * cosine[:, :k_cols]
        + mm((grad_k * sine[:, :k_cols]).astype(BF), turn[:k_cols, :k_cols])
    ).astype(BF)
    grad_qkv = jnp.concatenate([grad_q_low, grad_k_low, grad_v.astype(BF)], axis=1)
    w_qkv = jnp.concatenate([w_query, w_key, w_value], axis=1)
    input_part = mm_nt(grad_qkv, w_qkv)
    grad_normed_one = lax.psum_scatter(
        input_part.astype(BF), "tp", scatter_dimension=0, tiled=True
    ).astype(F32)
    scale_own = mine(scale_one)
    weighted_one = grad_normed_one * norm_attn
    grad_norm_attn = jnp.sum(input_part * x_full * scale_one, axis=0)
    tokens_own = (
        grad_residual
        + scale_own * weighted_one
        - x_own * scale_own**3 * jnp.mean(weighted_one * x_own, axis=1, keepdims=True)
    )
    grad_tokens = lax.all_gather(tokens_own.astype(BF), "tp", axis=0, tiled=True)
    small = jnp.concatenate([grad_router_part, grad_norm_moe[None]], axis=0)
    small = lax.psum(small, BOTH)
    grad_norm_attn = lax.psum(grad_norm_attn, BOTH)
    grad_w_out = lax.psum(grad_w_out.astype(BF), "ep").astype(F32)
    grad_w_qkv = lax.psum(mm_tn(normed_one, grad_qkv).astype(BF), "ep").astype(F32)
    return (
        output,
        grad_tokens,
        grad_norm_attn,
        grad_w_qkv[:, :q_cols],
        grad_w_qkv[:, q_cols : q_cols + k_cols],
        grad_w_qkv[:, q_cols + k_cols :],
        grad_w_out,
        small[experts],
        small[:experts].T,
        grad_expert_gate,
        grad_expert_up,
        grad_expert_down,
    )


def solution(mesh):
    in_specs = (
        P("ep", None),
        P(),
        P(None, "tp"),
        P(None, "tp"),
        P(None, "tp"),
        P("tp", None),
        P(),
        P(),
        P("ep", None, "tp"),
        P("ep", None, "tp"),
        P("ep", "tp", None),
        P("ep", None),
        P("ep", None),
        P("ep", None),
    )
    out_specs = (
        P("ep", None),
        P("ep", None),
        P(),
        P(None, "tp"),
        P(None, "tp"),
        P(None, "tp"),
        P("tp", None),
        P(),
        P(),
        P("ep", None, "tp"),
        P("ep", None, "tp"),
        P("ep", "tp", None),
    )
    return jax.shard_map(body, mesh=mesh, in_specs=in_specs, out_specs=out_specs, check_vma=False)
```

time: 1790 us -> 1030 us (0.58)
  waiting for transfers between devices: 1230 us -> 725 us
  local copies, waits for them, and re-layouts: 281 us -> 48.1 us
  other arithmetic: 84.6 us -> 20 us
  blocking collectives: 21.9 us -> 83.4 us
  starting transfers between devices: 23.1 us -> 1.13 us
    all_to_all x4 -> x0, waiting for transfers between devices: 621 us -> none  [the longest x2 415 us: to_experts(): return lax.all_to_all(buffer, 'ep', split_axis=0, concat_axis=1, tiled=True)]
    gather x10 -> x0, local copies, waits for them, and re-layouts: 177 us -> none  [the longest x2 54.4 us: to_experts(): picked = padded_rows[owner_token]]
    reduce_scatter x2 -> x5, waiting for transfers between devices: 339 us -> 433 us  [the longest x1 146 us: body(): lax.psum_scatter(row_part, BOTH, scatter_dimension=0, tiled=True)]
    all_to_all x4 -> x0, local copies, waits for them, and re-layouts: 43.7 us -> none  [the longest x2 26.2 us: to_sources(): return lax.all_to_all(joined, 'ep', split_axis=1, concat_axis=0, tiled=True)]
    all_gather x0 -> x1, blocking collectives: none -> 42.2 us  [body(): mask_all = lax.all_gather(mask_own.astype(BF), BOTH, axis=0, tiled=True)]
    psum x3 -> x2, waiting for transfers between devices: 118 us -> 160 us  [the longest x1 105 us: body(): small = lax.psum(small, BOTH)]
    all_gather x2 -> x0, local copies, waits for them, and re-layouts: 34.4 us -> none  [to_sources(): joined = lax.all_gather(summed, 'tp', axis=2, tiled=True)]
    convert_element_type x20 -> x8, other arithmetic: 38 us -> 11.2 us  [the longest x1 2.27 us: body(): grad_residual.astype(BF)]
  transfers between devices with their start and end apart: 11 -> 12, of which waited for: 11 -> 12; matrix products, arithmetic and copies ran while one was open for 17% -> 11% of each run, Pallas kernels for 0% -> 0%
where the time goes in v1:
time: 1030 us; the launch traced here: 1020 us
  waiting for transfers between devices  725 us (70%)
  matrix products  127 us (12%)
  blocking collectives  83.4 us (8%)
  local copies, waits for them, and re-layouts  48.1 us (5%)
  other arithmetic  20 us (2%)
  between operations  15.3 us (1%)
    reduce_scatter x1, waiting for transfers between devices, body(): lax.psum_scatter(row_part, BOTH, scatter_dimension=0, tiled=True)  146 us
    reduce_scatter x1, waiting for transfers between devices, body(): mixture = lax.psum_scatter(mix_part, BOTH, scatter_dimension=0, tiled=True)  145 us
    psum x1, waiting for transfers between devices, body(): small = lax.psum(small, BOTH)  105 us
    reduce_scatter x1, waiting for transfers between devices, body(): lax.psum_scatter(gates_dense, BOTH, scatter_dimension=0, tiled=True)  103 us
    all_gather x1, waiting for transfers between devices, body(): grad_all = lax.all_gather(grad_own, BOTH, axis=0, tiled=True)  60.5 us
    psum x1, waiting for transfers between devices, body(): lax.psum(mm_tn(normed_one, grad_qkv).astype(BF), 'ep').astype(F32)  54.1 us
    all_gather x1, blocking collectives, body(): mask_all = lax.all_gather(mask_own.astype(BF), BOTH, axis=0, tiled=True)  42.2 us
    psum x1, blocking collectives, body(): grad_norm_attn = lax.psum(grad_norm_attn, BOTH)  41.2 us
  transfers between devices with their start and end apart: 12, of which 12 were waited for; matrix products, arithmetic and copies ran while one was open for 11% of the time, Pallas kernels for 0%

profile of v1, /device:TPU:0, one launch (start us, length us, event | category | flops | bytes accessed | tf_op | source)
XLA Modules:
  0.0 1019.8 jit_solution(17315644787649215206)
XLA Ops:
  14.2 2.8 fusion.35
  26.6 4.6 fusion.63
  31.2 2.7 convolution_convert_fusion.4
  36.6 34.2 %reduce-scatter.6.cloned.1.call-done = f32[128,1024]{1,0:T(8,128)} async-done(((f32[512,1024]{1,0:T(8,128)}), f32[128,1024]{1,0:T(8,128)}) %reduce-scatter.6.cloned.1.call-update) | async-done | bytes 524304 | tf_op jit(solution)/shard_map/reduce_scatter | solution.py:162
  75.7 2.3 copy.110
  78.0 2.3 copy.109
  81.7 42.2 %all_gather.18 = bf16[4096,32]{0,1:T(8,128)(2,1)S(1)} all-gather(bf16[128,32]{0,1:T(8,128)(2,1)S(1)} %get-tuple-element.48), channel_id=1, replica_groups=mesh['ep'=8,'tp'=4] {'ep','tp'}, dimensions={0}, use_global_device_ids=true | all-gather | bytes 270336 | tf_op jit(solution)/shard_map/all_gather | solution.py:95
  124.0 28.5 %all-gather.6.cloned.1.call-done = bf16[4096,1024]{1,0:T(8,128)(2,1)} async-done(((bf16[128,1024]{1,0:T(8,128)(2,1)}), bf16[4096,1024]{1,0:T(8,128)(2,1)}) %all-gather.6.cloned.1.call-update) | async-done | bytes 8388624 | tf_op jit(solution)/shard_map/all_gather | solution.py:166
  152.5 6.1 select_reduce_fusion
  158.9 13.2 %fusion.14 = f32[4096,1024]{0,1:T(8,128)} fusion(bf16[4096,1024]{1,0:T(8,128)(2,1)S(1)} %copy-done.6, bf16[1024,512]{0,1:T(8,128)(2,1)S(1)} %bitcast.128, bf16[1024,512]{0,1:T(8,128)(2,1)S(1)} %bitcast.130), kind=kOutput, calls=%fused_computation.37 | convolution fusion | flops 8594128896 | bytes 27262976 | tf_op jit(solution)/shard_map/dot_general | solution.py:16
  172.1 60.5 %all-gather.10.cloned.1.call-done = bf16[4096,1024]{1,0:T(8,128)(2,1)} async-done(((bf16[128,1024]{1,0:T(8,128)(2,1)}), bf16[4096,1024]{1,0:T(8,128)(2,1)}) %all-gather.10.cloned.1.call-update) | async-done | bytes 8388624 | tf_op jit(solution)/shard_map/all_gather | solution.py:89
  238.7 17.9 %multiply_convert_fusion.1 = (bf16[4096,512]{0,1:T(8,128)(2,1)}, bf16[4096,512]{0,1:T(8,128)(2,1)}, f32[4096,512]{0,1:T(8,128)S(1)}) fusion(f32[4096,1024]{0,1:T(8,128)} %fusion.14, f32[4096,128]{0,1:T(8,128)} %broadcast_in_dim.126, f32[4096,128]{0,1:T(8,128)} %broadcast_in_dim.124, f32[4096,128]{0,1:T(8,128)} %broadcast_in_dim.122, ...), kind=kOutput, calls=%fused_computation.7 | convolution fusion | flops 4336910336 | bytes 51380224 | tf_op jit(solution)/shard_map/dot_general | solution.py:20
  258.9 15.1 %convolution_convert_fusion = bf16[4096,1024]{1,0:T(8,128)(2,1)} fusion(bf16[4096,512]{0,1:T(8,128)(2,1)} %get-tuple-element.31, bf16[4096,512]{0,1:T(8,128)(2,1)} %get-tuple-element.30, bf16[1024,512]{0,1:T(8,128)(2,1)} %bitcast.127, bf16[1024,512]{0,1:T(8,128)(2,1)} %bitcast.129), kind=kOutput, calls=%fused_computation.10 | convolution fusion | flops 8615100416 | bytes 18874368 | tf_op jit(solution)/shard_map/dot_general | solution.py:20
  274.0 13.1 %convolution_convert_fusion.1 = bf16[4096,1024]{1,0:T(8,128)(2,1)} fusion(bf16[512,1024]{1,0:T(8,128)(2,1)S(1)} %bitcast.112, f32[4096,128]{0,1:T(8,128)} %broadcast_in_dim.126, f32[4096,128]{0,1:T(8,128)} %broadcast_in_dim.124, f32[4096,128]{0,1:T(8,128)} %broadcast_in_dim.122, f32[4096,128]{0,1:T(8,128)} %broadcast_in_dim.120, f32[4096,1024]{0,1:T(8,128)} %fusion.14), kind=kOutput, calls=%fused_computation.11 | convolution fusion | flops 4320133120 | bytes 34603008 | tf_op jit(solution)/shard_map/dot_general | solution.py:16
  287.8 103.2 %reduce-scatter.12.cloned.1.call-done = f32[128,32]{0,1:T(8,128)} async-done(((f32[4096,32]{0,1:T(8,128)}), f32[128,32]{0,1:T(8,128)}) %reduce-scatter.12.cloned.1.call-update) | async-done | bytes 16400 | tf_op jit(solution)/shard_map/reduce_scatter | solution.py:206
  391.8 146.4 %reduce-scatter.10.cloned.1.call-done = bf16[128,1024]{1,0:T(8,128)(2,1)} async-done(((bf16[4096,1024]{1,0:T(8,128)(2,1)}), bf16[128,1024]{1,0:T(8,128)(2,1)}) %reduce-scatter.10.cloned.1.call-update) | async-done | bytes 262160 | tf_op jit(solution)/shard_map/reduce_scatter | solution.py:208
  540.3 144.8 %reduce-scatter.8.cloned.1.call-done = bf16[128,1024]{1,0:T(8,128)(2,1)} async-done(((bf16[4096,1024]{1,0:T(8,128)(2,1)}), bf16[128,1024]{1,0:T(8,128)(2,1)}) %reduce-scatter.8.cloned.1.call-update) | async-done | bytes 262160 | tf_op jit(solution)/shard_map/reduce_scatter | solution.py:210
  685.1 2.3 fusion.58
  687.7 12.5 %all-gather.12.cloned.1.call-done = bf16[512,1024]{1,0:T(8,128)(2,1)} async-done(((bf16[128,1024]{1,0:T(8,128)(2,1)}), bf16[512,1024]{1,0:T(8,128)(2,1)}) %all-gather.12.cloned.1.call-update) | async-done | bytes 1048592 | tf_op jit(solution)/shard_map/all_gather | solution.py:240
  701.9 3.8 convolution_convert_fusion.6
  718.6 3.1 fusion.10
  726.9 15.5 %fusion.54 = f32[512,1024]{1,0:T(8,128)} fusion(bf16[4096,1024]{1,0:T(8,128)(2,1)} %all-gather.10.cloned.1.call-done, f32[4096,128]{0,1:T(8,128)} %broadcast_in_dim.126, f32[4096,128]{0,1:T(8,128)} %broadcast_in_dim.124, f32[4096,128]{0,1:T(8,128)} %broadcast_in_dim.122, f32[4096,128]{0,1:T(8,128)} %broadcast_in_dim.120, f32[4096,1024]{0,1:T(8,128)} %fusion.14), kind=kOutput, calls=%fused_computation.143 | convolution fusion | flops 4315938816 | bytes 35651584 | tf_op jit(solution)/shard_map/dot_general | solution.py:24
  742.4 4.4 reduce-scatter.14.cloned.1.call-done
  749.8 14.0 %fusion.4 = f32[1024,1024]{0,1:T(8,128)S(1)} fusion(bf16[4096,1024]{1,0:T(8,128)(2,1)} %all-gather.6.cloned.1.call-done, bf16[4096,512]{0,1:T(8,128)(2,1)} %get-tuple-element.31, bf16[4096,512]{0,1:T(8,128)(2,1)} %get-tuple-element.30), kind=kOutput, calls=%fused_computation.12 | convolution fusion | flops 8606711808 | bytes 20971520 | tf_op jit(solution)/shard_map/dot_general | solution.py:24
  765.5 2.9 copy.131
  770.2 105.5 %all-reduce.4.cloned.1.call-done = f32[33,1024]{1,0:T(8,128)} async-done(((f32[33,1024]{1,0:T(8,128)}), f32[33,1024]{1,0:T(8,128)}) %all-reduce.4.cloned.1.call-update) | async-done | bytes 135184 | tf_op jit(solution)/shard_map/psum | solution.py:274
  878.6 17.3 %all-gather.8.cloned.1.call-done = bf16[512,1024]{1,0:T(8,128)(2,1)} async-done(((bf16[128,1024]{1,0:T(8,128)(2,1)}), bf16[512,1024]{1,0:T(8,128)(2,1)}) %all-gather.8.cloned.1.call-update) | async-done | bytes 1048592 | tf_op jit(solution)/shard_map/all_gather | solution.py:218
  895.9 41.2 %psum.28 = f32[1024]{0:T(1024)} all-reduce(f32[1024]{0:T(1024)S(1)} %get-tuple-element.35), channel_id=1, replica_groups=mesh['ep'=8,'tp'=4] {'ep','tp'}, use_global_device_ids=true, to_apply=%region_26.27 | all-reduce | flops 1024 | bytes 8192 | tf_op jit(solution)/shard_map/psum | solution.py:275
  937.1 54.1 %all-reduce.6.cloned.1.call-done = (bf16[1024,512]{1,0:T(8,128)(2,1)}, bf16[256,1024]{1,0:T(8,128)(2,1)}) async-done(((bf16[1024,512]{1,0:T(8,128)(2,1)}, bf16[256,1024]{1,0:T(8,128)(2,1)}), (bf16[1024,512]{1,0:T(8,128)(2,1)}, bf16[256,1024]{1,0:T(8,128)(2,1)})) %all-reduce.6.cloned.1.call-update) | async-done | bytes 1572880 | tf_op jit(solution)/shard_map/psum | solution.py:277
  991.2 2.2 slice.134
  996.6 12.8 %all-gather.14.cloned.1.call-done = bf16[512,1024]{1,0:T(8,128)(2,1)} async-done(((bf16[128,1024]{1,0:T(8,128)(2,1)}), bf16[512,1024]{1,0:T(8,128)(2,1)}) %all-gather.14.cloned.1.call-update) | async-done | bytes 1048592 | tf_op jit(solution)/shard_map/all_gather | solution.py:272
  1010.4 2.3 copy.157
  (212 shorter events, 70.9 us)
Async XLA Ops:
  7.2 231.5 %copy-start = (bf16[4,128,1024]{2,1,0:T(8,128)(2,1)S(1)}, bf16[4,128,1024]{2,1,0:T(8,128)(2,1)}, u32[]{:S(2)}) copy-start(bf16[4,128,1024]{2,1,0:T(8,128)(2,1)} %param.25) | copy-start | bytes 3145732
  7.2 63.6 %reduce-scatter.6.cloned.1.call-start = ((), (), s32[]{:S(2)}) async-start(), calls=%async_computation.5 | async-start | bytes 2621440 | tf_op jit(solution)/shard_map/reduce_scatter | solution.py:162
  21.5 9.7 copy-start.9
  34.0 36.9 %copy-start.15 = (bf16[512,1024]{1,0:T(8,128)(2,1)S(1)}, bf16[512,1024]{1,0:T(8,128)(2,1)}, u32[]{:S(2)}) copy-start(bf16[512,1024]{1,0:T(8,128)(2,1)} %param.15) | copy-start | bytes 3145732
  34.0 39.1 %copy-start.33 = (f32[1024]{0:T(1024)S(1)}, f32[1024]{0:T(1024)}, u32[]{:S(2)}) copy-start(f32[1024]{0:T(1024)} %param.21) | copy-start | bytes 12292
  36.6 44.4 %copy-start.26 = (bf16[1024,32]{0,1:T(8,128)(2,1)S(1)}, bf16[1024,32]{0,1:T(8,128)(2,1)}, u32[]{:S(2)}) copy-start(bf16[1024,32]{0,1:T(8,128)(2,1)} %param.22) | copy-start | bytes 196612
  36.6 115.9 %all-gather.6.cloned.1.call-start = ((), (), s32[]{:S(2)}) async-start(), calls=%async_computation.6 | async-start | bytes 8650752 | tf_op jit(solution)/shard_map/all_gather | solution.py:166
  73.9 158.6 %all-gather.10.cloned.1.call-start = ((), (), s32[]{:S(2)}) async-start(), calls=%async_computation.9 | async-start | bytes 8650752 | tf_op jit(solution)/shard_map/all_gather | solution.py:89
  75.7 315.4 %reduce-scatter.12.cloned.1.call-start = ((), (), s32[]{:S(2)}) async-start(), calls=%async_computation.11 | async-start | bytes 540672 | tf_op jit(solution)/shard_map/reduce_scatter | solution.py:206
  258.7 279.5 %reduce-scatter.10.cloned.1.call-start = ((), (), s32[]{:S(2)}) async-start(), calls=%async_computation.10 | async-start | bytes 8650752 | tf_op jit(solution)/shard_map/reduce_scatter | solution.py:208
  274.0 411.1 %reduce-scatter.8.cloned.1.call-start = ((), (), s32[]{:S(2)}) async-start(), calls=%async_computation.7 | async-start | bytes 8650752 | tf_op jit(solution)/shard_map/reduce_scatter | solution.py:210
  287.1 251.0 %copy-start.34 = (f32[1024]{0:T(1024)S(1)}, f32[1024]{0:T(1024)}, u32[]{:S(2)}) copy-start(f32[1024]{0:T(1024)} %param.21) | copy-start | bytes 12292
  287.2 251.0 %copy-start.47 = (f32[128]{0:T(128)S(1)}, f32[128]{0:T(128)}, u32[]{:S(2)}) copy-start(f32[128]{0:T(128)} %copy-done.46) | copy-start | bytes 1540
  287.2 397.9 %copy-start.50 = (f32[128]{0:T(128)S(1)}, f32[128]{0:T(128)}, u32[]{:S(2)}) copy-start(f32[128]{0:T(128)} %get-tuple-element.51) | copy-start | bytes 1540
  287.2 413.0 %copy-start.28 = (bf16[256,1024]{1,0:T(8,128)(2,1)S(1)}, bf16[256,1024]{1,0:T(8,128)(2,1)}, u32[]{:S(2)}) copy-start(bf16[256,1024]{1,0:T(8,128)(2,1)} %param.20) | copy-start | bytes 1572868
  287.2 414.7 %copy-start.41 = (f32[2,1024]{1,0:T(2,128)S(1)}, f32[2,1024]{1,0:T(2,128)}, u32[]{:S(2)}) copy-start(f32[2,1024]{1,0:T(2,128)} %copy-done.40) | copy-start | bytes 24580
  287.2 412.9 %all-gather.12.cloned.1.call-start = ((), (), s32[]{:S(2)}) async-start(), calls=%async_computation.12 | async-start | bytes 1310720 | tf_op jit(solution)/shard_map/all_gather | solution.py:240
  287.8 417.9 %copy-start.42 = (f32[128]{0:T(128)}, f32[128]{0:T(128)S(1)}, u32[]{:S(2)}) copy-start(f32[128]{0:T(128)S(1)} %fusion.40) | copy-start | bytes 1540
  391.8 313.9 %copy-start.44 = (f32[128]{0:T(128)}, f32[128]{0:T(128)S(1)}, u32[]{:S(2)}) copy-start(f32[128]{0:T(128)S(1)} %multiply_reduce_fusion.4) | copy-start | bytes 1540
  687.4 59.4 %reduce-scatter.14.cloned.1.call-start = ((), (), s32[]{:S(2)}) async-start(), calls=%async_computation.13 | async-start | bytes 1310720 | tf_op jit(solution)/shard_map/reduce_scatter | solution.py:261
  707.7 8.8 copy-start.3
  707.7 8.8 copy-start.5
  707.7 9.3 copy-start.8
  707.7 9.3 copy-start.10
  709.2 9.4 copy-start.49
  721.7 154.0 %all-reduce.4.cloned.1.call-start = ((), (), s32[]{:S(2)}) async-start(), calls=%async_computation.15 | async-start | bytes 327680 | tf_op jit(solution)/shard_map/psum | solution.py:274
  722.8 173.2 %all-gather.8.cloned.1.call-start = ((), (), s32[]{:S(2)}) async-start(), calls=%async_computation.8 | async-start | bytes 1310720 | tf_op jit(solution)/shard_map/all_gather | solution.py:218
  723.3 267.9 %all-reduce.6.cloned.1.call-start = ((), (), s32[]{:S(2)}) async-start(), calls=%async_computation.16 | async-start | bytes 3145728 | tf_op jit(solution)/shard_map/psum | solution.py:277
  726.6 21.3 %copy-start.18 = (f32[128,1024]{1,0:T(8,128)S(1)}, f32[128,1024]{1,0:T(8,128)}, u32[]{:S(2)}) copy-start(f32[128,1024]{1,0:T(8,128)} %get-tuple-element.23) | copy-start | bytes 1572868
  726.6 282.8 %all-gather.14.cloned.1.call-start = ((), (), s32[]{:S(2)}) async-start(), calls=%async_computation.14 | async-start | bytes 1310720 | tf_op jit(solution)/shard_map/all_gather | solution.py:272
  895.9 113.5 %copy-start.23 = (bf16[512,1024]{1,0:T(8,128)(2,1)S(1)}, bf16[512,1024]{1,0:T(8,128)(2,1)}, u32[]{:S(2)}) copy-start(bf16[512,1024]{1,0:T(8,128)(2,1)} %all-gather.8.cloned.1.call-done) | copy-start | bytes 3145732
  991.2 21.4 %copy-start.1 = (bf16[4,128,1024]{2,1,0:T(8,128)(2,1)S(1)}, bf16[4,128,1024]{2,1,0:T(8,128)(2,1)}, u32[]{:S(2)}) copy-start(bf16[4,128,1024]{2,1,0:T(8,128)(2,1)} %param.25) | copy-start | bytes 3145732
  (33 other events, 140.0 us)
Sparse Core Ops, SparseCore 0:
  36.7 34.0 reduce-scatter.5
  74.7 77.7 all-gather.5
  156.4 76.1 all-gather.9
  258.8 132.1 reduce-scatter.11
  393.2 144.9 reduce-scatter.9
  540.3 144.7 reduce-scatter.7
  687.5 12.5 all-gather.11
  721.8 24.8 reduce-scatter.13
  753.8 121.8 all-reduce.3
  877.2 18.7 all-gather.7
  900.6 90.6 all-reduce.5
  993.3 16.0 all-gather.13

commit v2 on v1

--- a/solution.py
+++ b/solution.py
@@ -7,7 +7,7 @@
 HEAD = 64
 EPSILON = 1e-06
 ROPE_BASE = 10000.0
-BOTH = ("ep", "tp")
+BOTH = ("tp", "ep")
 BF = jnp.bfloat16
 F32 = jnp.float32
 
@@ -69,6 +69,7 @@
     out_grad,
 ):
     highest = lax.Precision.HIGHEST
+    ep_size = lax.axis_size("ep")
     tok_rows, width = tokens.shape
     q_cols, k_cols = w_query.shape[1], w_key.shape[1]
     kv = k_cols // HEAD
@@ -85,6 +86,13 @@
     def mine(array):
         return lax.dynamic_slice_in_dim(array, first, own, 0)
 
+    def to_owners(parts):
+        over_tp = lax.psum_scatter(parts, "tp", scatter_dimension=0, tiled=True)
+        blocks = lax.all_to_all(
+            over_tp.reshape(ep_size, own, parts.shape[1]), "ep", split_axis=0, concat_axis=0
+        )
+        return jnp.sum(blocks.astype(F32), axis=0)
+
     grad_own = mine(out_grad)
     grad_all = lax.all_gather(grad_own, BOTH, axis=0, tiled=True)
     ids_own = mine(expert_ids)
@@ -92,7 +100,6 @@
         (ids_own[:, :, None] == jnp.arange(experts, dtype=jnp.int32)[None, None, :]).astype(F32),
         axis=1,
     )
-    mask_all = lax.all_gather(mask_own.astype(BF), BOTH, axis=0, tiled=True)
 
     w_gate_up = jnp.concatenate(
         [
@@ -159,19 +166,30 @@
     attended = flat_q(mixed.astype(BF))
     attn_partial = mm(attended, w_out)
     x_own = mine(tokens).astype(F32)
-    residual = x_own + lax.psum_scatter(attn_partial, "tp", scatter_dimension=0, tiled=True)
+    attn_partial, grad_all = lax.optimization_barrier((attn_partial.astype(BF), grad_all))
+    attn_sum = lax.psum_scatter(attn_partial, "tp", scatter_dimension=0, tiled=True)
+    residual = x_own + attn_sum.astype(F32)
     scale_two = lax.rsqrt(jnp.mean(residual * residual, axis=1, keepdims=True) + EPSILON)
     normed_two = (residual * scale_two * norm_moe).astype(BF)
 
-    rows_all = lax.all_gather(normed_two, BOTH, axis=0, tiled=True)
-    logits = mm(rows_all, router)
-    mask = mask_all > 0
-    masked = jnp.where(mask, logits, -jnp.inf)
-    chosen_exp = jnp.where(
-        mask, jnp.exp(logits - jnp.max(masked, axis=1, keepdims=True)), 0.0
-    )
-    gates_all = chosen_exp / jnp.sum(chosen_exp, axis=1, keepdims=True)
-    gates = lax.dynamic_slice_in_dim(gates_all, ep_at * local_experts, local_experts, 1)
+    logits = mm(normed_two, router)
+    keep = mask_own > 0
+    largest = jnp.max(jnp.where(keep, logits, -jnp.inf), axis=1, keepdims=True)
+    own_exp = jnp.where(keep, jnp.exp(logits - largest), 0.0)
+    gates_own = own_exp / jnp.sum(own_exp, axis=1, keepdims=True)
+    gates_high = gates_own.astype(BF)
+    gates_rest = (gates_own - gates_high.astype(F32)).astype(BF)
+
+    lanes = -(-2 * experts // 128) * 128
+    sent = jnp.concatenate(
+        [normed_two, gates_high, gates_rest, jnp.zeros((own, lanes - 2 * experts), BF)], axis=1
+    )
+    sent_all = lax.all_gather(sent, BOTH, axis=0, tiled=True)
+    rows_all = sent_all[:, :width]
+    gates_all = sent_all[:, width:].astype(F32)
+    gates = lax.dynamic_slice_in_dim(
+        gates_all, ep_at * local_experts, local_experts, 1
+    ) + lax.dynamic_slice_in_dim(gates_all, experts + ep_at * local_experts, local_experts, 1)
     all_rows = rows_all.shape[0]
     wide = local_experts * ff
     gate_wide = jnp.concatenate(
@@ -201,35 +219,28 @@
         axis=1,
     )
     gates_dense = lax.dynamic_update_slice_in_dim(
-        jnp.zeros((all_rows, experts), F32), grad_gates_part, ep_at * local_experts, 1
-    )
-    grad_gates = lax.psum_scatter(gates_dense, BOTH, scatter_dimension=0, tiled=True)
-    row_part = mm_nt(grad_pre, w_gate_up).astype(BF)
-    row_grads = lax.psum_scatter(row_part, BOTH, scatter_dimension=0, tiled=True)
+        jnp.zeros((all_rows, lanes), BF),
+        grad_gates_part.astype(BF),
+        ep_at * local_experts,
+        1,
+    )
+    row_part = jnp.concatenate([mm_nt(grad_pre, w_gate_up).astype(BF), gates_dense], axis=1)
+    row_sums = to_owners(row_part)
+    row_grads = row_sums[:, :width]
+    grad_gates = row_sums[:, width : width + experts]
     mix_part = mm(weighted, w_down).astype(BF)
-    mixture = lax.psum_scatter(mix_part, BOTH, scatter_dimension=0, tiled=True)
     grad_w_gu = mm_tn(rows_all, grad_pre)
     grad_w_gu = grad_w_gu.reshape(width, 2, local_experts, ff)
     grad_expert_gate = grad_w_gu[:, 0].transpose(1, 0, 2)
     grad_expert_up = grad_w_gu[:, 1].transpose(1, 0, 2)
     grad_expert_down = mm_tn(weighted, grad_all).reshape(local_experts, ff, width)
 
-    output_own = (residual + mixture.astype(F32)).astype(BF)
-    output = lax.all_gather(output_own, "tp", axis=0, tiled=True)
-    logits_own = mm(normed_two, router)
-    keep = mask_own > 0
-    own_exp = jnp.where(
-        keep,
-        jnp.exp(logits_own - jnp.max(jnp.where(keep, logits_own, -jnp.inf), axis=1, keepdims=True)),
-        0.0,
-    )
-    gates_own = own_exp / jnp.sum(own_exp, axis=1, keepdims=True)
     grad_logits = gates_own * (
         grad_gates - jnp.sum(gates_own * grad_gates, axis=1, keepdims=True)
     )
     grad_router_part = jnp.dot(grad_logits.T, normed_two.astype(F32), precision=highest)
     router_input = jnp.dot(grad_logits, router.astype(F32).T, precision=highest)
-    grad_normed_two = row_grads.astype(F32) + router_input
+    grad_normed_two = row_grads + router_input
     weighted_two = grad_normed_two * norm_moe
     grad_norm_moe = jnp.sum(grad_normed_two * residual * scale_two, axis=0)
     grad_residual = (
@@ -237,7 +248,22 @@
         + scale_two * weighted_two
         - residual * scale_two**3 * jnp.mean(weighted_two * residual, axis=1, keepdims=True)
     )
-    grad_attn = lax.all_gather(grad_residual.astype(BF), "tp", axis=0, tiled=True)
+    below = -(-(experts + 1) // 16) * 16
+    sent_attn = jnp.concatenate(
+        [
+            grad_residual.astype(BF),
+            grad_router_part.astype(BF),
+            grad_norm_moe[None].astype(BF),
+            jnp.zeros((below - experts - 1, width), BF),
+        ],
+        axis=0,
+    )
+    gathered = lax.all_gather(sent_attn, "tp", axis=0, tiled=False)
+    grad_attn = gathered[:, :own].reshape(tok_rows, width)
+    small = jnp.sum(gathered[:, own:].astype(F32), axis=0)
+    mix_part, grad_attn = lax.optimization_barrier((mix_part, grad_attn))
+    mixture = to_owners(mix_part)
+    output_own = (residual + mixture).astype(BF)
     grad_w_out = mm_tn(attended, grad_attn)
 
     grad_attended = heads_q(mm_nt(grad_attn, w_out).astype(BF))
@@ -258,22 +284,39 @@
     grad_qkv = jnp.concatenate([grad_q_low, grad_k_low, grad_v.astype(BF)], axis=1)
     w_qkv = jnp.concatenate([w_query, w_key, w_value], axis=1)
     input_part = mm_nt(grad_qkv, w_qkv)
-    grad_normed_one = lax.psum_scatter(
-        input_part.astype(BF), "tp", scatter_dimension=0, tiled=True
-    ).astype(F32)
+    norm_part = jnp.sum(input_part * x_full * scale_one, axis=0, keepdims=True)
+    extra = jnp.concatenate([norm_part.astype(BF), jnp.zeros((15, width), BF)], axis=0)
+    input_sent = jnp.concatenate(
+        [
+            input_part.astype(BF).reshape(tp_size, own, width),
+            jnp.broadcast_to(extra[None], (tp_size, 16, width)),
+        ],
+        axis=1,
+    )
+    input_sums = lax.psum_scatter(
+        input_sent.reshape(tp_size * (own + 16), width), "tp", scatter_dimension=0, tiled=True
+    )
+    grad_normed_one = input_sums[:own].astype(F32)
+    grad_norm_attn = input_sums[own:]
     scale_own = mine(scale_one)
     weighted_one = grad_normed_one * norm_attn
-    grad_norm_attn = jnp.sum(input_part * x_full * scale_one, axis=0)
     tokens_own = (
         grad_residual
         + scale_own * weighted_one
         - x_own * scale_own**3 * jnp.mean(weighted_one * x_own, axis=1, keepdims=True)
     )
-    grad_tokens = lax.all_gather(tokens_own.astype(BF), "tp", axis=0, tiled=True)
-    small = jnp.concatenate([grad_router_part, grad_norm_moe[None]], axis=0)
-    small = lax.psum(small, BOTH)
-    grad_norm_attn = lax.psum(grad_norm_attn, BOTH)
-    grad_w_out = lax.psum(grad_w_out.astype(BF), "ep").astype(F32)
+    both = lax.all_gather(
+        jnp.concatenate([output_own, tokens_own.astype(BF)], axis=0), "tp", axis=0, tiled=False
+    )
+    output = both[:, :own].reshape(tok_rows, width)
+    grad_tokens = both[:, own:].reshape(tok_rows, width)
+    stacked = jnp.concatenate(
+        [grad_w_out.astype(BF), small.astype(BF), grad_norm_attn], axis=0
+    )
+    stacked = lax.psum(stacked, "ep").astype(F32)
+    grad_w_out = stacked[: w_out.shape[0]]
+    small = stacked[w_out.shape[0] : w_out.shape[0] + below]
+    grad_norm_attn = stacked[w_out.shape[0] + below]
     grad_w_qkv = lax.psum(mm_tn(normed_one, grad_qkv).astype(BF), "ep").astype(F32)
     return (
         output,

time: 1030 us -> 685 us (0.67)
  waiting for transfers between devices: 725 us -> 443 us
  blocking collectives: 83.4 us -> 0 us
  other arithmetic: 20 us -> 32 us
  starting transfers between devices: 1.13 us -> 12.3 us
    reduce_scatter x4 -> x3, waiting for transfers between devices: 399 us -> 144 us  [the longest x2 127 us: to_owners(): over_tp = lax.psum_scatter(parts, 'tp', scatter_dimension=0, tiled=True)]
    psum x2 -> x1, waiting for transfers between devices: 160 us -> 37.1 us  [body(): stacked = lax.psum(stacked, 'ep').astype(F32)]
    all_to_all x0 -> x2, waiting for transfers between devices: none -> 78.4 us  [to_owners(): lax.all_to_all(over_tp.reshape(ep_size, own, parts.shape[1]), 'ep', split...]
    all_gather x1 -> x0, blocking collectives: 42.2 us -> none  [body(): mask_all = lax.all_gather(mask_own.astype(BF), BOTH, axis=0, tiled=True)]
    psum x1 -> x0, blocking collectives: 41.2 us -> none  [body(): grad_norm_attn = lax.psum(grad_norm_attn, BOTH)]
    all_gather x4 -> x3, waiting for transfers between devices: 71.1 us -> 99.4 us  [the longest x1 79.4 us: body(): sent_all = lax.all_gather(sent, BOTH, axis=0, tiled=True)]
    concatenate x1 -> x5, other arithmetic: 0.68 us -> 12 us  [the longest x1 7.28 us: body(): jnp.concatenate([mm_nt(grad_pre, w_gate_up).astype(BF), gates_dense], axi...]
    all_to_all x0 -> x2, starting transfers between devices: none -> 11.2 us  [to_owners(): lax.all_to_all(over_tp.reshape(ep_size, own, parts.shape[1]), 'ep', split...]
  transfers between devices with their start and end apart: 12 -> 11, of which waited for: 12 -> 11; matrix products, arithmetic and copies ran while one was open for 11% -> 18% of each run, Pallas kernels for 0% -> 0%
where the time goes in v2:
time: 685 us; the launch traced here: 678 us
  waiting for transfers between devices  443 us (65%)
  matrix products  120 us (18%)
  local copies, waits for them, and re-layouts  55.9 us (8%)
  other arithmetic  32 us (5%)
  between operations  15 us (2%)
  starting transfers between devices  12.3 us (2%)
    reduce_scatter x2, waiting for transfers between devices, to_owners(): over_tp = lax.psum_scatter(parts, 'tp', scatter_dimension=0, tiled=True)  127 us
    all_gather x1, waiting for transfers between devices, body(): sent_all = lax.all_gather(sent, BOTH, axis=0, tiled=True)  79.4 us
    all_to_all x2, waiting for transfers between devices, to_owners(): lax.all_to_all(over_tp.reshape(ep_size, own, parts.shape[1]), 'ep', split...  78.4 us
    all_gather x1, waiting for transfers between devices, body(): grad_all = lax.all_gather(grad_own, BOTH, axis=0, tiled=True)  57.9 us
    psum x1, waiting for transfers between devices, body(): stacked = lax.psum(stacked, 'ep').astype(F32)  37.1 us
    dot_general x4, matrix products, mm_tn(): lax.dot_general(a, b, (((0,), (0,)), ((), ())), preferred_element_type=F32)  35.7 us
    dot_general x7, matrix products, mm(): return jnp.dot(a, b, preferred_element_type=F32)  32.4 us
    dot_general x4, matrix products, mm_nt(): lax.dot_general(a, b, (((1,), (1,)), ((), ())), preferred_element_type=F32)  32.3 us
  transfers between devices with their start and end apart: 11, of which 11 were waited for; matrix products, arithmetic and copies ran while one was open for 18% of the time, Pallas kernels for 0%

profile of v2, /device:TPU:0, one launch (start us, length us, event | category | flops | bytes accessed | tf_op | source)
XLA Modules:
  0.0 677.8 jit_solution(17134920638565269872)
XLA Ops:
  25.1 3.6 fusion.64
  28.8 2.7 convolution_convert_fusion.5
  33.7 57.9 %all-gather.7.cloned.1.call-done = bf16[4096,1024]{1,0:T(8,128)(2,1)} async-done(((bf16[128,1024]{1,0:T(8,128)(2,1)}), bf16[4096,1024]{1,0:T(8,128)(2,1)}) %all-gather.7.cloned.1.call-update) | async-done | bytes 8388624 | tf_op jit(solution)/shard_map/all_gather | solution.py:97
  92.5 25.7 %reduce-scatter.5.cloned.1.call-done = bf16[128,1024]{1,0:T(8,128)(2,1)} async-done(((bf16[512,1024]{1,0:T(8,128)(2,1)}), bf16[128,1024]{1,0:T(8,128)(2,1)}) %reduce-scatter.5.cloned.1.call-update) | async-done | bytes 262160 | tf_op jit(solution)/shard_map/reduce_scatter | solution.py:170
  126.7 79.4 %all-gather.9.cloned.1.call-done = bf16[4096,1152]{1,0:T(8,128)(2,1)} async-done(((bf16[128,1152]{1,0:T(8,128)(2,1)}), bf16[4096,1152]{1,0:T(8,128)(2,1)}) %all-gather.9.cloned.1.call-update) | async-done | bytes 9437200 | tf_op jit(solution)/shard_map/all_gather | solution.py:187
  208.6 3.9 slice_reduce_fusion.7
  212.5 12.8 %fusion.6 = f32[4096,1024]{0,1:T(8,128)} fusion(bf16[4096,1152]{1,0:T(8,128)(2,1)S(1)} %copy-done.37, bf16[1024,512]{0,1:T(8,128)(2,1)S(1)} %bitcast.138, bf16[1024,512]{0,1:T(8,128)(2,1)S(1)} %bitcast.135), kind=kOutput, calls=%fused_computation.15 | convolution fusion | flops 8594128896 | bytes 27262976 | tf_op jit(solution)/shard_map/dot_general | solution.py:16
  231.4 17.8 %multiply_convert_fusion.1 = (bf16[4096,512]{0,1:T(8,128)(2,1)}, bf16[4096,512]{0,1:T(8,128)(2,1)}, f32[4096,512]{0,1:T(8,128)S(1)}) fusion(f32[4096,1024]{0,1:T(8,128)} %fusion.6, f32[4096,128]{0,1:T(8,128)} %broadcast_in_dim.131, f32[4096,128]{0,1:T(8,128)} %broadcast_in_dim.129, f32[4096,128]{0,1:T(8,128)} %broadcast_in_dim.127, ...), kind=kOutput, calls=%fused_computation.8 | convolution fusion | flops 4336910336 | bytes 51380224 | tf_op jit(solution)/shard_map/dot_general | solution.py:20
  249.8 11.9 %convolution_convert_fusion = bf16[4096,1024]{0,1:T(8,128)(2,1)S(1)} fusion(bf16[4096,512]{0,1:T(8,128)(2,1)} %get-tuple-element.42, bf16[4096,512]{0,1:T(8,128)(2,1)} %get-tuple-element.41, bf16[1024,512]{0,1:T(8,128)(2,1)} %bitcast.137, bf16[1024,512]{0,1:T(8,128)(2,1)S(1)} %bitcast.136), kind=kOutput, calls=%fused_computation.11 | convolution fusion | flops 8615100416 | bytes 18874368 | tf_op jit(solution)/shard_map/dot_general | solution.py:20
  261.9 7.3 %pad_maximum_fusion = bf16[4096,1152]{0,1:T(8,128)(2,1)} fusion(bf16[4096,128]{0,1:T(8,128)(2,1)S(1)} %maximum_dynamic-update-slice_fusion, bf16[4096,1024]{0,1:T(8,128)(2,1)S(1)} %convolution_convert_fusion), kind=kLoop, calls=%fused_computation.1 | loop fusion | flops 18874368 | bytes 18874368 | tf_op jit(solution)/shard_map/concatenate | solution.py:227
  269.2 77.2 %reduce-scatter.7.cloned.1.call-done = bf16[1024,1152]{0,1:T(8,128)(2,1)} async-done(((bf16[4096,1152]{0,1:T(8,128)(2,1)}), bf16[1024,1152]{0,1:T(8,128)(2,1)}) %reduce-scatter.7.cloned.1.call-update) | async-done | bytes 2359312 | tf_op jit(solution)/shard_map/reduce_scatter | solution.py:90
  346.4 3.5 copy_bitcast_fusion
  349.9 5.7 all-to-all-start
  356.2 53.2 %all-to-all-done = bf16[8,128,1152]{1,2,0:T(8,128)(2,1)S(1)} async-done(((bf16[8,128,1152]{1,2,0:T(8,128)(2,1)}), bf16[8,128,1152]{1,2,0:T(8,128)(2,1)S(1)}, u32[]{:S(2)}, u32[]{:S(2)}) %all-to-all-start) | async-done | bytes 2359328 | tf_op jit(solution)/shard_map/all_to_all | solution.py:91
  416.4 13.8 %convolution_convert_fusion.1 = bf16[4096,1024]{1,0:T(8,128)(2,1)} fusion(bf16[512,1024]{1,0:T(8,128)(2,1)S(1)} %bitcast.113, f32[4096,128]{0,1:T(8,128)} %broadcast_in_dim.131, f32[4096,128]{0,1:T(8,128)} %broadcast_in_dim.129, f32[4096,128]{0,1:T(8,128)} %broadcast_in_dim.127, f32[4096,128]{0,1:T(8,128)} %broadcast_in_dim.125, f32[4096,1024]{0,1:T(8,128)} %fusion.6), kind=kOutput, calls=%fused_computation.12 | convolution fusion | flops 4320133120 | bytes 34603008 | tf_op jit(solution)/shard_map/dot_general | solution.py:16
  430.2 3.3 all-gather.11.cloned.1.call-done
  436.8 3.1 multiply_reduce_fusion
  445.6 4.8 convolution_convert_fusion.7
  457.7 50.2 %reduce-scatter.9.cloned.1.call-done = bf16[1024,1024]{1,0:T(8,128)(2,1)} async-done(((bf16[4096,1024]{1,0:T(8,128)(2,1)}), bf16[1024,1024]{1,0:T(8,128)(2,1)}) %reduce-scatter.9.cloned.1.call-update) | async-done | bytes 2097168 | tf_op jit(solution)/shard_map/reduce_scatter | solution.py:90
  507.9 5.5 all-to-all-start.1
  514.6 2.5 convolution_convert_fusion.4
  517.2 2.9 convolution_convert_fusion.3
  520.1 16.7 %reduce-scatter.11.cloned.1.call-done = bf16[144,1024]{1,0:T(8,128)(2,1)} async-done(((bf16[576,1024]{1,0:T(8,128)(2,1)}), bf16[144,1024]{1,0:T(8,128)(2,1)}) %reduce-scatter.11.cloned.1.call-update) | async-done | bytes 294928 | tf_op jit(solution)/shard_map/reduce_scatter | solution.py:296
  539.7 15.1 %fusion.4 = f32[1024,1024]{0,1:T(8,128)} fusion(bf16[4096,1152]{1,0:T(8,128)(2,1)} %all-gather.9.cloned.1.call-done, bf16[4096,512]{0,1:T(8,128)(2,1)} %get-tuple-element.42, bf16[4096,512]{0,1:T(8,128)(2,1)} %get-tuple-element.41), kind=kOutput, calls=%fused_computation.13 | convolution fusion | flops 8606711808 | bytes 20971520 | tf_op jit(solution)/shard_map/dot_general | solution.py:24
  555.0 25.2 %all-to-all-done.1 = bf16[8,128,1024]{2,1,0:T(8,128)(2,1)S(1)} async-done(((bf16[8,128,1024]{2,1,0:T(8,128)(2,1)}), bf16[8,128,1024]{2,1,0:T(8,128)(2,1)S(1)}, u32[]{:S(2)}, u32[]{:S(2)}) %all-to-all-start.1) | async-done | bytes 2097184 | tf_op jit(solution)/shard_map/all_to_all | solution.py:91
  582.8 4.0 fusion.59
  586.8 2.9 copy.182
  591.5 15.2 %fusion.53 = f32[512,1024]{1,0:T(8,128)} fusion(bf16[4096,1024]{1,0:T(8,128)(2,1)} %all-gather.7.cloned.1.call-done, f32[4096,128]{0,1:T(8,128)} %broadcast_in_dim.131, f32[4096,128]{0,1:T(8,128)} %broadcast_in_dim.129, f32[4096,128]{0,1:T(8,128)} %broadcast_in_dim.127, f32[4096,128]{0,1:T(8,128)} %broadcast_in_dim.125, f32[4096,1024]{0,1:T(8,128)} %fusion.6), kind=kOutput, calls=%fused_computation.158 | convolution fusion | flops 4315938816 | bytes 35651584 | tf_op jit(solution)/shard_map/dot_general | solution.py:24
  606.7 37.1 %all-reduce.4.cloned.1.call-done = (bf16[320,1024]{1,0:T(8,128)(2,1)}, bf16[1024,512]{1,0:T(8,128)(2,1)}) async-done(((bf16[320,1024]{1,0:T(8,128)(2,1)}, bf16[1024,512]{1,0:T(8,128)(2,1)}), (bf16[320,1024]{1,0:T(8,128)(2,1)}, bf16[1024,512]{1,0:T(8,128)(2,1)})) %all-reduce.4.cloned.1.call-update) | async-done | bytes 1703952 | tf_op jit(solution)/shard_map/psum | solution.py:316
  645.1 2.1 slice.199
  651.3 16.7 %all-gather.13.cloned.1.call-done = bf16[1024,1024]{1,0:T(8,128)(2,1)} async-done(((bf16[256,1024]{1,0:T(8,128)(2,1)}), bf16[1024,1024]{1,0:T(8,128)(2,1)}) %all-gather.13.cloned.1.call-update) | async-done | bytes 2097168 | tf_op jit(solution)/shard_map/all_gather | solution.py:308
  668.0 3.0 fusion.60
  (220 shorter events, 76.0 us)
Async XLA Ops:
  7.2 224.2 %copy-start = (bf16[4,128,1024]{2,1,0:T(8,128)(2,1)S(1)}, bf16[4,128,1024]{2,1,0:T(8,128)(2,1)}, u32[]{:S(2)}) copy-start(bf16[4,128,1024]{2,1,0:T(8,128)(2,1)} %param.25) | copy-start | bytes 3145732
  7.2 84.4 %all-gather.7.cloned.1.call-start = ((), (), s32[]{:S(2)}) async-start(), calls=%async_computation.6 | async-start | bytes 8650752 | tf_op jit(solution)/shard_map/all_gather | solution.py:97
  9.0 109.2 %reduce-scatter.5.cloned.1.call-start = ((), (), s32[]{:S(2)}) async-start(), calls=%async_computation.7 | async-start | bytes 1310720 | tf_op jit(solution)/shard_map/reduce_scatter | solution.py:170
  15.9 7.0 %copy-start.2 = (f32[512,32]{1,0:T(8,128)}, f32[512,32]{1,0:T(8,128)S(1)}, u32[]{:S(2)}) copy-start(f32[512,32]{1,0:T(8,128)S(1)} %get-tuple-element.60) | copy-start | bytes 196612
  15.9 7.0 %copy-start.4 = (f32[512,32]{1,0:T(8,128)}, f32[512,32]{1,0:T(8,128)S(1)}, u32[]{:S(2)}) copy-start(f32[512,32]{1,0:T(8,128)S(1)} %get-tuple-element.61) | copy-start | bytes 196612
  22.9 5.8 copy-start.22
  28.7 91.1 %copy-start.40 = (f32[1024]{0:T(1024)S(1)}, f32[1024]{0:T(1024)}, u32[]{:S(2)}) copy-start(f32[1024]{0:T(1024)} %param.21) | copy-start | bytes 12292
  31.5 89.4 %copy-start.38 = (bf16[1024,32]{0,1:T(8,128)(2,1)S(1)}, bf16[1024,32]{0,1:T(8,128)(2,1)}, u32[]{:S(2)}) copy-start(bf16[1024,32]{0,1:T(8,128)(2,1)} %param.22) | copy-start | bytes 196612
  31.5 92.5 %copy-start.23 = (bf16[4,1024,128]{2,1,0:T(8,128)(2,1)S(1)}, bf16[4,1024,128]{2,1,0:T(8,128)(2,1)}, u32[]{:S(2)}) copy-start(bf16[4,1024,128]{2,1,0:T(8,128)(2,1)} %param.23) | copy-start | bytes 3145732
  91.6 114.4 %all-gather.9.cloned.1.call-start = ((), (), s32[]{:S(2)}) async-start(), calls=%async_computation.8 | async-start | bytes 9732096 | tf_op jit(solution)/shard_map/all_gather | solution.py:187
  121.0 86.4 %copy-start.18 = (bf16[128,1024]{1,0:T(8,128)(2,1)}, bf16[128,1024]{1,0:T(8,128)(2,1)S(1)}, u32[]{:S(2)}) copy-start(bf16[128,1024]{1,0:T(8,128)(2,1)S(1)} %multiply_convert_fusion.4) | copy-start | bytes 786436
  123.8 222.6 %reduce-scatter.7.cloned.1.call-start = ((), (), s32[]{:S(2)}) async-start(), calls=%async_computation.9 | async-start | bytes 11796480 | tf_op jit(solution)/shard_map/reduce_scatter | solution.py:90
  349.9 61.7 %copy-start.39 = (bf16[1024,32]{0,1:T(8,128)(2,1)S(1)}, bf16[1024,32]{0,1:T(8,128)(2,1)}, u32[]{:S(2)}) copy-start(bf16[1024,32]{0,1:T(8,128)(2,1)} %param.22) | copy-start | bytes 196612
  349.9 59.5 %all-to-all-start = ((bf16[8,128,1152]{1,2,0:T(8,128)(2,1)}), bf16[8,128,1152]{1,2,0:T(8,128)(2,1)S(1)}, u32[]{:S(2)}, u32[]{:S(2)}) async-start(bf16[8,128,1152]{1,2,0:T(8,128)(2,1)} %copy_bitcast_fusion), calls=%async_computation.2 | async-start | bytes 4718592 | tf_op jit(solution)/shard_map/all_to_all | solution.py:91
  355.6 77.9 %all-gather.11.cloned.1.call-start = ((), (), s32[]{:S(2)}) async-start(), calls=%async_computation.12 | async-start | bytes 1802240 | tf_op jit(solution)/shard_map/all_gather | solution.py:261
  409.8 5.6 copy-start.45
  416.3 91.6 %reduce-scatter.9.cloned.1.call-start = ((), (), s32[]{:S(2)}) async-start(), calls=%async_computation.10 | async-start | bytes 10485760 | tf_op jit(solution)/shard_map/reduce_scatter | solution.py:90
  434.9 101.9 %reduce-scatter.11.cloned.1.call-start = ((), (), s32[]{:S(2)}) async-start(), calls=%async_computation.11 | async-start | bytes 1474560 | tf_op jit(solution)/shard_map/reduce_scatter | solution.py:296
  445.6 5.9 copy-start.3
  445.6 5.9 copy-start.5
  445.6 7.6 %copy-start.11 = (f32[512,256]{1,0:T(8,128)S(1)}, f32[512,256]{1,0:T(8,128)}, u32[]{:S(2)}) copy-start(f32[512,256]{1,0:T(8,128)} %concatenate.60) | copy-start | bytes 1572868
  445.6 7.6 %copy-start.13 = (f32[512,256]{1,0:T(8,128)S(1)}, f32[512,256]{1,0:T(8,128)}, u32[]{:S(2)}) copy-start(f32[512,256]{1,0:T(8,128)} %concatenate.61) | copy-start | bytes 1572868
  445.6 7.6 %copy-start.19 = (f32[512,256]{1,0:T(8,128)S(1)}, f32[512,256]{1,0:T(8,128)}, u32[]{:S(2)}) copy-start(f32[512,256]{1,0:T(8,128)} %copy.161) | copy-start | bytes 1572868
  445.6 8.8 %copy-start.7 = (bf16[512,1024]{1,0:T(8,128)(2,1)S(1)}, bf16[512,1024]{1,0:T(8,128)(2,1)}, u32[]{:S(2)}) copy-start(bf16[512,1024]{1,0:T(8,128)(2,1)} %param.15) | copy-start | bytes 3145732
  445.6 8.8 %copy-start.44 = (f32[512]{0:T(512)S(1)}, f32[512]{0:T(512)}, u32[]{:S(2)}) copy-start(f32[512]{0:T(512)} %copy-done.43) | copy-start | bytes 6148
  457.7 59.4 %copy-start.8 = (bf16[512,1024]{1,0:T(8,128)(2,1)S(1)}, bf16[512,1024]{1,0:T(8,128)(2,1)}, u32[]{:S(2)}) copy-start(bf16[512,1024]{1,0:T(8,128)(2,1)} %param.15) | copy-start | bytes 3145732
  457.7 59.4 %copy-start.42 = (f32[1024]{0:T(1024)S(1)}, f32[1024]{0:T(1024)}, u32[]{:S(2)}) copy-start(f32[1024]{0:T(1024)} %param.16) | copy-start | bytes 12292
  507.9 72.3 %all-to-all-start.1 = ((bf16[8,128,1024]{2,1,0:T(8,128)(2,1)}), bf16[8,128,1024]{2,1,0:T(8,128)(2,1)S(1)}, u32[]{:S(2)}, u32[]{:S(2)}) async-start(bf16[8,128,1024]{2,1,0:T(8,128)(2,1)} %bitcast.123), calls=%async_computation.4 | async-start | bytes 4194304 | tf_op jit(solution)/shard_map/all_to_all | solution.py:91
  513.4 130.3 %all-reduce.4.cloned.1.call-start = ((), (), s32[]{:S(2)}) async-start(), calls=%async_computation.14 | async-start | bytes 3407872 | tf_op jit(solution)/shard_map/psum | solution.py:316
  539.5 128.5 %all-gather.13.cloned.1.call-start = ((), (), s32[]{:S(2)}) async-start(), calls=%async_computation.13 | async-start | bytes 2621440 | tf_op jit(solution)/shard_map/all_gather | solution.py:308
  539.7 15.1 %copy-start.21 = (bf16[144,1024]{1,0:T(8,128)(2,1)S(1)}, bf16[144,1024]{1,0:T(8,128)(2,1)}, u32[]{:S(2)}) copy-start(bf16[144,1024]{1,0:T(8,128)(2,1)} %reduce-scatter.11.cloned.1.call-done) | copy-start | bytes 884740
  647.2 23.8 %copy-start.1 = (bf16[4,128,1024]{2,1,0:T(8,128)(2,1)S(1)}, bf16[4,128,1024]{2,1,0:T(8,128)(2,1)}, u32[]{:S(2)}) copy-start(bf16[4,128,1024]{2,1,0:T(8,128)(2,1)} %param.25) | copy-start | bytes 3145732
  (26 other events, 74.5 us)
Sparse Core Ops, SparseCore 0:
  11.6 79.9 all-gather.6
  94.7 23.4 reduce-scatter.4
  123.9 82.0 all-gather.8
  269.3 77.0 reduce-scatter.6
  416.4 17.0 all-gather.10
  436.1 71.7 reduce-scatter.8
  511.0 25.7 reduce-scatter.10
  541.5 102.2 all-reduce.3
  645.9 22.0 all-gather.12
